TPU v7x, 256 devices: a whole 4x4x8 slice. The times are simulated.
256 devices in a mesh: cyc: 16 (over y, x), row: 4 (over z_hi), col: 4 (over z_lo, core).
Axes of the slice: x: 4, y: 4, z: 8 (z_hi: 4, z_lo: 2; z = z_hi * 2 + z_lo), core: 2. Of those that a mesh axis runs over, the one named last changes fastest.
Arguments:
- raw: bfloat16 [32, 4, 1024, 2048], P('cyc', None, 'row', 'col'), may hold values from 0.099609375 to 4
- flat: float32 [4, 1024, 2048], P(None, 'row', 'col'), may hold values from 0.5 to 2
- dark: float32 [4, 1024, 2048], P(None, 'row', 'col'), may hold values from 0 to 1
- shifts: int32 [32, 8, 16, 2], P('cyc', 'row', 'col'), may hold values from -48 to 48, as said below
- fractions: int32 [32, 8, 16, 2], P('cyc', 'row', 'col'), may hold values from 0 to 7
Outputs:
- registered: bfloat16 [32, 4, 1024, 2048], P('cyc', None, 'row', 'col')
- scores: float32 [32, 32, 64], P('cyc', 'row', 'col')
Inputs may be any that keep to these rules, and one draw needn't show every extreme that they name: `shifts`: each shift lies within 48 pixels; both ends are taken in every draw.
All inputs are finite; a program needn't handle non-finite values.
Results may differ from a plain program's by a relative error of at most 0.0041.
Values may be sent and summed in bfloat16 or wider, within the bound.
A program may use at most 128 MiB of HBM per device.

v0:
```python
import jax
import jax.numpy as jnp
from jax import lax
from jax.sharding import PartitionSpec as P

TILE = 128
RADIUS = 4
SHIFT = 48
BOX = 32


def padded(block, sides, width):
    for axis, dim in sides:
        count = lax.axis_size(axis)
        forward = [(i, i + 1) for i in range(count - 1)]
        backward = [(target, source) for source, target in forward]
        low = lax.ppermute(
            lax.slice_in_dim(block, block.shape[dim] - width, None, axis=dim), axis, forward
        )
        high = lax.ppermute(lax.slice_in_dim(block, 0, width, axis=dim), axis, backward)
        block = jnp.concatenate([low, block, high], axis=dim)
    return block


def from_root(block, axis, holder):
    block = jnp.where(lax.axis_index(axis) == holder, block, jnp.zeros_like(block))
    return lax.psum(block, axis)


def square_filter(image, start, combine):
    side = 2 * RADIUS + 1
    strides = (1, 1, 1, 1)
    along_cols = lax.reduce_window(
        image, jnp.array(start, image.dtype), combine, (1, 1, 1, side), strides, "VALID"
    )
    return lax.reduce_window(
        along_cols, jnp.array(start, image.dtype), combine, (1, 1, side, 1), strides, "VALID"
    )


def background(extended):
    eroded = square_filter(extended, jnp.inf, lax.min)
    opened = square_filter(eroded, -jnp.inf, lax.max)
    margin = 2 * RADIUS
    inner = extended[:, :, margin : extended.shape[2] - margin, margin : extended.shape[3] - margin]
    return inner - opened


def one_tile(image, row_start, col_start, frac_row, frac_col):
    zero = jnp.zeros((), jnp.int32)
    block = lax.dynamic_slice(
        image, (zero, row_start, col_start), (image.shape[0], TILE + 1, TILE + 1)
    ).astype(jnp.float32)
    lower = frac_row.astype(jnp.float32) / 8.0
    right = frac_col.astype(jnp.float32) / 8.0
    rows_mixed = block[:, :TILE, :] * (1.0 - lower) + block[:, 1:, :] * lower
    return rows_mixed[:, :, :TILE] * (1.0 - right) + rows_mixed[:, :, 1:] * right


def resample(pulled, shifts, fractions):
    cycles_here = shifts.shape[0]
    tile_rows = shifts.shape[1]
    tile_cols = shifts.shape[2]
    margin = SHIFT + 1
    base_rows = jnp.arange(tile_rows, dtype=jnp.int32)[:, None] * TILE + margin
    base_cols = jnp.arange(tile_cols, dtype=jnp.int32)[None, :] * TILE + margin
    row_start = (base_rows[None] + shifts[..., 0]).reshape(cycles_here, -1)
    col_start = (base_cols[None] + shifts[..., 1]).reshape(cycles_here, -1)
    frac_row = fractions[..., 0].reshape(cycles_here, -1)
    frac_col = fractions[..., 1].reshape(cycles_here, -1)
    per_image = jax.vmap(one_tile, in_axes=(None, 0, 0, 0, 0))
    tiles = jax.vmap(per_image)(pulled, row_start, col_start, frac_row, frac_col)
    channels = pulled.shape[1]
    tiles = tiles.reshape(cycles_here, tile_rows, tile_cols, channels, TILE, TILE)
    whole = tiles.transpose(0, 3, 1, 4, 2, 5).reshape(
        cycles_here, channels, tile_rows * TILE, tile_cols * TILE
    )
    return whole.astype(jnp.bfloat16)


def box_scores(moving, fixed):
    lead = moving.shape[0]
    first = moving.astype(jnp.float32).reshape(
        lead, moving.shape[1] // BOX, BOX, moving.shape[2] // BOX, BOX
    )
    second = fixed.astype(jnp.float32).reshape(
        1, fixed.shape[0] // BOX, BOX, fixed.shape[1] // BOX, BOX
    )
    first = first - jnp.mean(first, axis=(2, 4), keepdims=True)
    second = second - jnp.mean(second, axis=(2, 4), keepdims=True)
    covar = jnp.mean(first * second, axis=(2, 4))
    var_first = jnp.mean(first * first, axis=(2, 4))
    var_second = jnp.mean(second * second, axis=(2, 4))
    return covar / jnp.sqrt(var_first * var_second + 1e-06)


def body(raw, flat, dark, shifts, fractions):
    corrected = (raw.astype(jnp.float32) - dark[None]) / flat[None]
    extended = padded(corrected, (("row", 2), ("col", 3)), 2 * RADIUS)
    tophat = background(extended).astype(jnp.bfloat16)
    pulled = padded(tophat, (("row", 2), ("col", 3)), SHIFT + 1)
    registered = resample(pulled, shifts, fractions)
    panel = from_root(registered[0, 0], "cyc", 0)
    scores = box_scores(registered[:, 0], panel)
    return (registered, scores)


def solution(mesh):
    return jax.shard_map(
        body,
        mesh=mesh,
        in_specs=(
            P("cyc", None, "row", "col"),
            P(None, "row", "col"),
            P(None, "row", "col"),
            P("cyc", "row", "col", None),
            P("cyc", "row", "col", None),
        ),
        out_specs=(P("cyc", None, "row", "col"), P("cyc", "row", "col")),
        check_vma=False,
    )
```

profile of v0, /device:TPU:1, one launch (start us, length us, event | category | flops | bytes accessed | tf_op | source)
XLA Modules:
  0.0 365.6 jit_solution(13687392382428029934)
XLA Ops:
  12.8 5.7 %collective-permute-start = (f32[2,4,8,512]{3,2,1,0:T(8,128)S(1)}, f32[2,4,8,512]{3,2,1,0:T(8,128)S(1)}, u32[]{:S(2)}, u32[]{:S(2)}) collective-permute-start(f32[2,4,8,512]{3,2,1,0:T(8,128)S(1)} %get-tuple-element.33), channel_id=1, source_target_pairs={{0,4},{4,8},{8,12},{1,5},{5,9},{9,13},{2,6},{6,10},{10,14},{3,7},{... | collective-permute-start | bytes 393224 | tf_op jit(solution)/shard_map/ppermute | solution.py:17
  20.7 10.3 %collective-permute-done.1 = f32[2,4,8,512]{3,2,1,0:T(8,128)S(1)} collective-permute-done((f32[2,4,8,512]{3,2,1,0:T(8,128)S(1)}, f32[2,4,8,512]{3,2,1,0:T(8,128)S(1)}, u32[]{:S(2)}, u32[]{:S(2)}) %collective-permute-start.1) | collective-permute-done | bytes 131104 | tf_op jit(solution)/shard_map/ppermute | solution.py:20
  42.0 6.3 %pad_maximum_fusion = f32[2,4,272,528]{3,2,1,0:T(8,128)} fusion(f32[2,4,272,8]{3,2,1,0:T(8,128)S(1)} %copy.20, f32[2,4,8,512]{3,2,1,0:T(8,128)S(1)} %collective-permute-done.1, f32[2,4,256,512]{3,2,1,0:T(8,128)} %copy-done, f32[2,4,8,512]{3,2,1,0:T(8,128)S(1)} %collective-permute-done, f32[2,4,272,8]{3,2,1,0:T(8,128)S(1)} %copy.19), kind=kLoop, calls=%fused_computation.5 | loop fusion | flops 4595712 | bytes 9191424 | tf_op jit(solution)/shard_map/concatenate | solution.py:21
  48.3 20.5 %reduce_window.28 = f32[2,4,272,520]{3,2,1,0:T(8,128)} reduce-window(f32[2,4,272,528]{3,2,1,0:T(8,128)} %pad_maximum_fusion, f32[]{:T(128)} %constant.16.clone.1), window={size=1x1x1x9}, to_apply=%region_0.0 | reduce-window | flops 9052160 | bytes 9121796 | tf_op jit(solution)/shard_map/reduce_window | solution.py:33
  68.8 15.8 %reduce_window.29 = f32[2,4,264,520]{3,2,1,0:T(8,128)} reduce-window(f32[2,4,272,520]{3,2,1,0:T(8,128)} %reduce_window.28, f32[]{:T(128)} %constant.16.clone.1), window={size=1x1x9x1}, to_apply=%region_1.0 | reduce-window | flops 8785920 | bytes 8919044 | tf_op jit(solution)/shard_map/reduce_window | solution.py:36
  84.6 20.1 %reduce_window.30 = f32[2,4,264,512]{3,2,1,0:T(8,128)} reduce-window(f32[2,4,264,520]{3,2,1,0:T(8,128)} %reduce_window.29, f32[]{:T(128)} %constant.17.clone.1), window={size=1x1x1x9}, to_apply=%region_2.0 | reduce-window | flops 8650752 | bytes 8718340 | tf_op jit(solution)/shard_map/reduce_window | solution.py:33
  104.8 12.7 %reduce_window.31 = f32[2,4,256,512]{3,2,1,0:T(8,128)} reduce-window(f32[2,4,264,512]{3,2,1,0:T(8,128)} %reduce_window.30, f32[]{:T(128)} %constant.17.clone.1), window={size=1x1x9x1}, to_apply=%region_3.0 | reduce-window | flops 8388608 | bytes 8519684 | tf_op jit(solution)/shard_map/reduce_window | solution.py:36
  117.5 5.4 %subtract_convert_fusion = bf16[2,4,256,512]{3,2,1,0:T(8,128)(2,1)S(1)} fusion(f32[2,4,256,512]{3,2,1,0:T(8,128)} %reduce_window.31, f32[4,256,512]{2,1,0:T(8,128)} %param.6, f32[4,256,512]{2,1,0:T(8,128)} %param.7, bf16[2,4,256,512]{3,2,1,0:T(8,128)(2,1)} %param.5), kind=kLoop, calls=%fused_computation.12 | loop fusion | flops 5242880 | bytes 12582912 | tf_op jit(solution)/shard_map/convert_element_type | solution.py:100
  123.2 6.6 %collective-permute-start.4 = (bf16[2,4,49,512]{3,1,2,0:T(4,128)(2,1)S(1)}, bf16[2,4,49,512]{3,1,2,0:T(4,128)(2,1)S(1)}, u32[]{:S(2)}, u32[]{:S(2)}) collective-permute-start(bf16[2,4,49,512]{3,1,2,0:T(4,128)(2,1)S(1)} %copy.21), channel_id=1, source_target_pairs={{0,4},{4,8},{8,12},{1,5},{5,9},{9,13},{2,6},{6,10},{10,14},{3,7},{... | collective-permute-start | bytes 1204232 | tf_op jit(solution)/shard_map/ppermute | solution.py:17
  131.4 5.3 %collective-permute-done.4 = bf16[2,4,49,512]{3,1,2,0:T(4,128)(2,1)S(1)} collective-permute-done((bf16[2,4,49,512]{3,1,2,0:T(4,128)(2,1)S(1)}, bf16[2,4,49,512]{3,1,2,0:T(4,128)(2,1)S(1)}, u32[]{:S(2)}, u32[]{:S(2)}) %collective-permute-start.4) | collective-permute-done | bytes 401440 | tf_op jit(solution)/shard_map/ppermute | solution.py:17
  136.8 10.6 %collective-permute-done.5 = bf16[2,4,49,512]{3,1,2,0:T(4,128)(2,1)S(1)} collective-permute-done((bf16[2,4,49,512]{3,1,2,0:T(4,128)(2,1)S(1)}, bf16[2,4,49,512]{3,1,2,0:T(4,128)(2,1)S(1)}, u32[]{:S(2)}, u32[]{:S(2)}) %collective-permute-start.5) | collective-permute-done | bytes 401440 | tf_op jit(solution)/shard_map/ppermute | solution.py:20
  150.4 4.6 %collective-permute-start.6 = (bf16[2,4,354,49]{2,1,3,0:T(4,128)(2,1)S(1)}, bf16[2,4,354,49]{2,1,3,0:T(4,128)(2,1)}, u32[]{:S(2)}, u32[]{:S(2)}) collective-permute-start(bf16[2,4,354,49]{2,1,3,0:T(4,128)(2,1)S(1)} %copy.25), channel_id=1, source_target_pairs={{0,1},{1,2},{2,3},{4,5},{5,6},{6,7},{8,9},{9,10},{10,11},{12,13},{... | collective-permute-start | bytes 832616 | tf_op jit(solution)/shard_map/ppermute | solution.py:17
  161.7 3.8 %collective-permute-done.7 = bf16[2,4,354,49]{2,1,3,0:T(4,128)(2,1)} collective-permute-done((bf16[2,4,354,49]{2,1,3,0:T(4,128)(2,1)}, bf16[2,4,354,49]{2,1,3,0:T(4,128)(2,1)}, u32[]{:S(2)}, u32[]{:S(2)}) %collective-permute-start.7) | collective-permute-done | bytes 277568 | tf_op jit(solution)/shard_map/ppermute | solution.py:20
  167.7 6.1 %pad_maximum_fusion.1 = bf16[2,4,354,610]{3,2,1,0:T(8,128)(2,1)} fusion(bf16[2,4,354,49]{3,2,1,0:T(8,128)(2,1)} %copy.28, bf16[2,4,49,512]{3,2,1,0:T(8,128)(2,1)S(1)} %copy.24, bf16[2,4,256,512]{3,2,1,0:T(8,128)(2,1)S(1)} %subtract_convert_fusion, bf16[2,4,49,512]{3,2,1,0:T(8,128)(2,1)S(1)} %copy.23, bf16[2,4,354,49]{3,2,1,0:T(8,128)(2,1)} %copy.27), kind=kLoop, calls=%fused_computation.14 | loop fusion | flops 17275200 | bytes 6910080 | tf_op jit(solution)/shard_map/concatenate | solution.py:21
  173.8 71.5 %while.1 = (s32[]{:T(128)}, bf16[2,4,354,610]{3,2,1,0:T(8,128)(2,1)}, s32[16,4]{0,1:T(4,128)S(1)}, bf16[16,4,129,129]{3,2,1,0:T(8,128)(2,1)}, s32[]{:T(128)}) while((s32[]{:T(128)}, bf16[2,4,354,610]{3,2,1,0:T(8,128)(2,1)}, s32[16,4]{0,1:T(4,128)S(1)}, bf16[16,4,129,129]{3,2,1,0:T(8,128)(2,1)}, s32[]{:T(128)}) %tuple.33), condition=%wide.while_cond, body=%wide.while_body.sunk | while | flops 2 | bytes 559225 | solution.py:51
  174.4 3.8 %dynamic-slice_dynamic-update-slice_fusion.2 = bf16[16,4,129,129]{3,2,1,0:T(8,128)(2,1)} fusion(bf16[16,4,129,129]{3,2,1,0:T(8,128)(2,1)} %get-tuple-element.80, s32[]{:T(128)} %get-tuple-element.77, bf16[2,4,354,610]{3,2,1,0:T(8,128)(2,1)} %get-tuple-element.83, s32[]{:T(128)} %bitcast.17, s32[]{:T(128)} %bitcast.18, s32[]{:T(128)} %bitcast.19), kind=kLoop, calls=%fused_computation.clone.1 | loop fusion | bytes 559104 | tf_op jit(solution)/shard_map/vmap(vmap())/gather
  183.4 3.8 %dynamic-slice_dynamic-update-slice_fusion.2 = bf16[16,4,129,129]{3,2,1,0:T(8,128)(2,1)} fusion(bf16[16,4,129,129]{3,2,1,0:T(8,128)(2,1)} %get-tuple-element.80, s32[]{:T(128)} %get-tuple-element.77, bf16[2,4,354,610]{3,2,1,0:T(8,128)(2,1)} %get-tuple-element.83, s32[]{:T(128)} %bitcast.17, s32[]{:T(128)} %bitcast.18, s32[]{:T(128)} %bitcast.19), kind=kLoop, calls=%fused_computation.clone.1 | loop fusion | bytes 559104 | tf_op jit(solution)/shard_map/vmap(vmap())/gather
  196.8 3.8 %dynamic-slice_dynamic-update-slice_fusion.2 = bf16[16,4,129,129]{3,2,1,0:T(8,128)(2,1)} fusion(bf16[16,4,129,129]{3,2,1,0:T(8,128)(2,1)} %get-tuple-element.80, s32[]{:T(128)} %get-tuple-element.77, bf16[2,4,354,610]{3,2,1,0:T(8,128)(2,1)} %get-tuple-element.83, s32[]{:T(128)} %bitcast.17, s32[]{:T(128)} %bitcast.18, s32[]{:T(128)} %bitcast.19), kind=kLoop, calls=%fused_computation.clone.1 | loop fusion | bytes 559104 | tf_op jit(solution)/shard_map/vmap(vmap())/gather
  210.1 3.8 %dynamic-slice_dynamic-update-slice_fusion.2 = bf16[16,4,129,129]{3,2,1,0:T(8,128)(2,1)} fusion(bf16[16,4,129,129]{3,2,1,0:T(8,128)(2,1)} %get-tuple-element.80, s32[]{:T(128)} %get-tuple-element.77, bf16[2,4,354,610]{3,2,1,0:T(8,128)(2,1)} %get-tuple-element.83, s32[]{:T(128)} %bitcast.17, s32[]{:T(128)} %bitcast.18, s32[]{:T(128)} %bitcast.19), kind=kLoop, calls=%fused_computation.clone.1 | loop fusion | bytes 559104 | tf_op jit(solution)/shard_map/vmap(vmap())/gather
  219.1 3.8 %dynamic-slice_dynamic-update-slice_fusion.2 = bf16[16,4,129,129]{3,2,1,0:T(8,128)(2,1)} fusion(bf16[16,4,129,129]{3,2,1,0:T(8,128)(2,1)} %get-tuple-element.80, s32[]{:T(128)} %get-tuple-element.77, bf16[2,4,354,610]{3,2,1,0:T(8,128)(2,1)} %get-tuple-element.83, s32[]{:T(128)} %bitcast.17, s32[]{:T(128)} %bitcast.18, s32[]{:T(128)} %bitcast.19), kind=kLoop, calls=%fused_computation.clone.1 | loop fusion | bytes 559104 | tf_op jit(solution)/shard_map/vmap(vmap())/gather
  228.0 3.8 %dynamic-slice_dynamic-update-slice_fusion.2 = bf16[16,4,129,129]{3,2,1,0:T(8,128)(2,1)} fusion(bf16[16,4,129,129]{3,2,1,0:T(8,128)(2,1)} %get-tuple-element.80, s32[]{:T(128)} %get-tuple-element.77, bf16[2,4,354,610]{3,2,1,0:T(8,128)(2,1)} %get-tuple-element.83, s32[]{:T(128)} %bitcast.17, s32[]{:T(128)} %bitcast.18, s32[]{:T(128)} %bitcast.19), kind=kLoop, calls=%fused_computation.clone.1 | loop fusion | bytes 559104 | tf_op jit(solution)/shard_map/vmap(vmap())/gather
  232.5 3.8 %dynamic-slice_dynamic-update-slice_fusion.2 = bf16[16,4,129,129]{3,2,1,0:T(8,128)(2,1)} fusion(bf16[16,4,129,129]{3,2,1,0:T(8,128)(2,1)} %get-tuple-element.80, s32[]{:T(128)} %get-tuple-element.77, bf16[2,4,354,610]{3,2,1,0:T(8,128)(2,1)} %get-tuple-element.83, s32[]{:T(128)} %bitcast.17, s32[]{:T(128)} %bitcast.18, s32[]{:T(128)} %bitcast.19), kind=kLoop, calls=%fused_computation.clone.1 | loop fusion | bytes 559104 | tf_op jit(solution)/shard_map/vmap(vmap())/gather
  237.0 3.8 %dynamic-slice_dynamic-update-slice_fusion.2 = bf16[16,4,129,129]{3,2,1,0:T(8,128)(2,1)} fusion(bf16[16,4,129,129]{3,2,1,0:T(8,128)(2,1)} %get-tuple-element.80, s32[]{:T(128)} %get-tuple-element.77, bf16[2,4,354,610]{3,2,1,0:T(8,128)(2,1)} %get-tuple-element.83, s32[]{:T(128)} %bitcast.17, s32[]{:T(128)} %bitcast.18, s32[]{:T(128)} %bitcast.19), kind=kLoop, calls=%fused_computation.clone.1 | loop fusion | bytes 559104 | tf_op jit(solution)/shard_map/vmap(vmap())/gather
  263.6 83.8 %all-reduce.2.cloned.1.call-done = bf16[256,512]{1,0:T(8,128)(2,1)} async-done(((bf16[256,512]{1,0:T(8,128)(2,1)}), bf16[256,512]{1,0:T(8,128)(2,1)}) %all-reduce.2.cloned.1.call-update) | async-done | bytes 262160 | tf_op jit(solution)/shard_map/psum | solution.py:27
  (117 shorter events, 103.0 us)
Async XLA Ops:
  7.2 12.7 %copy-start.3 = (s32[2,2,4,2]{2,3,1,0:T(2,128)S(1)}, s32[2,2,4,2]{2,3,1,0:T(2,128)}, u32[]{:S(2)}) copy-start(s32[2,2,4,2]{2,3,1,0:T(2,128)} %param.8) | copy-start | bytes 388
  7.2 340.2 %all-reduce.2.cloned.1.call-start = ((), (), s32[]{:S(2)}) async-start(), calls=%async_computation | async-start | bytes 524288 | tf_op jit(solution)/shard_map/psum | solution.py:27
  10.8 2.0 copy-start
  12.8 7.9 %collective-permute-start = (f32[2,4,8,512]{3,2,1,0:T(8,128)S(1)}, f32[2,4,8,512]{3,2,1,0:T(8,128)S(1)}, u32[]{:S(2)}, u32[]{:S(2)}) collective-permute-start(f32[2,4,8,512]{3,2,1,0:T(8,128)S(1)} %get-tuple-element.33), channel_id=1, source_target_pairs={{0,4},{4,8},{8,12},{1,5},{5,9},{9,13},{2,6},{6,10},{10,14},{3,7},{... | collective-permute-start | bytes 393224 | tf_op jit(solution)/shard_map/ppermute | solution.py:17
  18.6 12.4 %collective-permute-start.1 = (f32[2,4,8,512]{3,2,1,0:T(8,128)S(1)}, f32[2,4,8,512]{3,2,1,0:T(8,128)S(1)}, u32[]{:S(2)}, u32[]{:S(2)}) collective-permute-start(f32[2,4,8,512]{3,2,1,0:T(8,128)S(1)} %get-tuple-element.34), channel_id=1, source_target_pairs={{4,0},{8,4},{12,8},{5,1},{9,5},{13,9},{6,2},{10,6},{14,10},{7,3},{... | collective-permute-start | bytes 393224 | tf_op jit(solution)/shard_map/ppermute | solution.py:20
  20.3 17.8 %copy-start.4 = (s32[2,2,4,2]{2,3,1,0:T(2,128)S(1)}, s32[2,2,4,2]{2,3,1,0:T(2,128)}, u32[]{:S(2)}) copy-start(s32[2,2,4,2]{2,3,1,0:T(2,128)} %param.9) | copy-start | bytes 388
  33.4 4.9 %collective-permute-start.2 = (f32[2,4,272,8]{2,3,1,0:T(8,128)S(1)}, f32[2,4,272,8]{2,3,1,0:T(8,128)S(1)}, u32[]{:S(2)}, u32[]{:S(2)}) collective-permute-start(f32[2,4,272,8]{2,3,1,0:T(8,128)S(1)} %copy.17), channel_id=1, source_target_pairs={{0,1},{1,2},{2,3},{4,5},{5,6},{6,7},{8,9},{9,10},{10,11},{12,13},{... | collective-permute-start | bytes 208904 | tf_op jit(solution)/shard_map/ppermute | solution.py:17
  35.7 5.9 %collective-permute-start.3 = (f32[2,4,272,8]{2,3,1,0:T(8,128)S(1)}, f32[2,4,272,8]{2,3,1,0:T(8,128)S(1)}, u32[]{:S(2)}, u32[]{:S(2)}) collective-permute-start(f32[2,4,272,8]{2,3,1,0:T(8,128)S(1)} %copy.18), channel_id=1, source_target_pairs={{1,0},{2,1},{3,2},{5,4},{6,5},{7,6},{9,8},{10,9},{11,10},{13,12},{... | collective-permute-start | bytes 208904 | tf_op jit(solution)/shard_map/ppermute | solution.py:20
  123.2 13.5 %collective-permute-start.4 = (bf16[2,4,49,512]{3,1,2,0:T(4,128)(2,1)S(1)}, bf16[2,4,49,512]{3,1,2,0:T(4,128)(2,1)S(1)}, u32[]{:S(2)}, u32[]{:S(2)}) collective-permute-start(bf16[2,4,49,512]{3,1,2,0:T(4,128)(2,1)S(1)} %copy.21), channel_id=1, source_target_pairs={{0,4},{4,8},{8,12},{1,5},{5,9},{9,13},{2,6},{6,10},{10,14},{3,7},{... | collective-permute-start | bytes 1204232 | tf_op jit(solution)/shard_map/ppermute | solution.py:17
  130.0 17.3 %collective-permute-start.5 = (bf16[2,4,49,512]{3,1,2,0:T(4,128)(2,1)S(1)}, bf16[2,4,49,512]{3,1,2,0:T(4,128)(2,1)S(1)}, u32[]{:S(2)}, u32[]{:S(2)}) collective-permute-start(bf16[2,4,49,512]{3,1,2,0:T(4,128)(2,1)S(1)} %copy.22), channel_id=1, source_target_pairs={{4,0},{8,4},{12,8},{5,1},{9,5},{13,9},{6,2},{10,6},{14,10},{7,3},{... | collective-permute-start | bytes 1204232 | tf_op jit(solution)/shard_map/ppermute | solution.py:20
  150.4 9.1 %collective-permute-start.6 = (bf16[2,4,354,49]{2,1,3,0:T(4,128)(2,1)S(1)}, bf16[2,4,354,49]{2,1,3,0:T(4,128)(2,1)}, u32[]{:S(2)}, u32[]{:S(2)}) collective-permute-start(bf16[2,4,354,49]{2,1,3,0:T(4,128)(2,1)S(1)} %copy.25), channel_id=1, source_target_pairs={{0,1},{1,2},{2,3},{4,5},{5,6},{6,7},{8,9},{9,10},{10,11},{12,13},{... | collective-permute-start | bytes 832616 | tf_op jit(solution)/shard_map/ppermute | solution.py:17
  157.1 8.4 %collective-permute-start.7 = (bf16[2,4,354,49]{2,1,3,0:T(4,128)(2,1)}, bf16[2,4,354,49]{2,1,3,0:T(4,128)(2,1)}, u32[]{:S(2)}, u32[]{:S(2)}) collective-permute-start(bf16[2,4,354,49]{2,1,3,0:T(4,128)(2,1)} %copy.26), channel_id=1, source_target_pairs={{1,0},{2,1},{3,2},{5,4},{6,5},{7,6},{9,8},{10,9},{11,10},{13,12},{... | collective-permute-start | bytes 832616 | tf_op jit(solution)/shard_map/ppermute | solution.py:20
  347.4 3.5 copy-start.2
  350.9 3.8 %copy-start.1 = (f32[8,32,16,32]{3,2,1,0:T(8,128)S(1)}, f32[8,32,16,32]{3,2,1,0:T(8,128)}, u32[]{:S(2)}) copy-start(f32[8,32,16,32]{3,2,1,0:T(8,128)} %broadcast_subtract_fusion) | copy-start | bytes 1572868
Sparse Core Ops, SparseCore 0:
  257.5 89.8 all-reduce.1
where the time goes:
time: 368 us; the launch traced here: 366 us
  waiting for transfers between devices  117 us (32%)
  other arithmetic  114 us (31%)
  local copies, waits for them, and re-layouts  94.4 us (26%)
  starting transfers between devices  26 us (7%)
  between operations  14.3 us (4%)
    psum x1, waiting for transfers between devices, from_root(): return lax.psum(block, axis)  83.8 us
    gather x48, local copies, waits for them, and re-layouts  71.4 us
    another operation x2, other arithmetic, square_filter(): lax.reduce_window(image, jnp.array(start, image.dtype), combine, (1, 1, 1...  40.6 us
    another operation x2, other arithmetic, square_filter(): lax.reduce_window(along_cols, jnp.array(start, image.dtype), combine, (1,...  28.5 us
    ppermute x4, waiting for transfers between devices, padded(): lax.ppermute(lax.slice_in_dim(block, 0, width, axis=dim), axis, backward)  27.8 us
    ppermute x4, starting transfers between devices, padded(): lax.ppermute(lax.slice_in_dim(block, block.shape[dim] - width, None, axis...  18.8 us
    concatenate x2, other arithmetic, padded(): block = jnp.concatenate([low, block, high], axis=dim)  12.4 us
  transfers between devices with their start and end apart: 9, of which 7 were waited for; matrix products, arithmetic and copies ran while one was open for 3% of the time, Pallas kernels for 0%

commit v1 on v0

v1 whole, which is shorter than its diff:
```python
import functools
import math

import jax
import jax.numpy as jnp
from jax import lax
from jax.experimental import pallas as pl
from jax.experimental.pallas import tpu as pltpu
from jax.sharding import PartitionSpec as P

TILE = 128
MARGIN = 8
ABOVE = 48
BELOW = 64
BOX = 32
LAG = 3
MESH = pl.DeviceIdType.MESH
F32 = jnp.float32
BF16 = jnp.bfloat16


def lane_iota(rows):
    return lax.broadcasted_iota(jnp.int32, (rows, TILE), 1)


def shifted(tiles, step):
    count = len(tiles)
    rolled = [pltpu.roll(tile, (-step) % TILE, 1) for tile in tiles]
    lane = lane_iota(tiles[0].shape[0])
    if step > 0:
        return [jnp.where(lane < TILE - step, rolled[t], rolled[(t + 1) % count]) for t in range(count)]
    return [jnp.where(lane >= -step, rolled[t], rolled[(t - 1) % count]) for t in range(count)]


def lane_window(tiles, combine, outputs):
    ahead, behind = shifted(tiles, 1), shifted(tiles, -1)
    three = [combine(combine(a, b), c) for a, b, c in zip(tiles, ahead, behind)]
    ahead, behind = shifted(three, 3), shifted(three, -3)
    return [combine(combine(three[t], ahead[t]), behind[t]) for t in range(outputs)]


def kernel(
    sizes, raw, flat, dark, shifts, fractions, out, scores,
    rawv, flatv, darkv, corr, pack_l, pack_r, halo_l, halo_r, tmp1, tmp2, hat, mixed, weights, reg, panel,
    sums, means,
    in_sem, out_sem, p_send, p_recv, c_send, c_recv, r_send, r_recv, h_send, h_recv, b_send, b_recv,
):
    n_cyc, n_row, n_col, nx = sizes
    ny = n_cyc // nx
    channels, rows, cols = flat.shape
    images = raw.shape[0] * channels
    lanes = cols // TILE
    cyc, row, col = lax.axis_index("cyc"), lax.axis_index("row"), lax.axis_index("col")
    yy, xx = cyc // nx, cyc % nx
    has_up, has_down = row > 0, row < n_row - 1
    has_left, has_right = col > 0, col < n_col - 1
    up, down = {"row": row - 1}, {"row": row + 1}
    left, right = {"col": col - 1}, {"col": col + 1}

    def in_copies(k):
        return (
            pltpu.make_async_copy(raw.at[:, k], rawv.at[:, k], in_sem.at[k, 0]),
            pltpu.make_async_copy(flat.at[k], flatv.at[k], in_sem.at[k, 1]),
            pltpu.make_async_copy(dark.at[k], darkv.at[k], in_sem.at[k, 2]),
        )

    for k in range(channels):
        for copy in in_copies(k):
            copy.start()

    barrier = pltpu.get_barrier_semaphore()

    def greet(device):
        pl.semaphore_signal(barrier, inc=1, device_id=device, device_id_type=MESH)

    for there, device in ((has_up, up), (has_down, down), (has_left, left), (has_right, right)):
        pl.when(there)(functools.partial(greet, device))
    for k in range(1, nx):
        pl.when(cyc == 0)(functools.partial(greet, {"cyc": k}))
    pl.when((yy == 0) & (xx > 0))(functools.partial(greet, {"cyc": 0}))
    for k in range(1, ny):
        pl.when(yy == 0)(functools.partial(greet, {"cyc": k * nx + xx}))
    pl.when(yy > 0)(functools.partial(greet, {"cyc": xx}))

    @pl.when(jnp.logical_not(has_up))
    def _():
        corr[:, :, 0:MARGIN, :] = jnp.zeros((images, lanes + 1, MARGIN, TILE), F32)
        hat[:, :, 0:ABOVE, :] = jnp.zeros((images, lanes + 2, ABOVE, TILE), BF16)

    @pl.when(jnp.logical_not(has_down))
    def _():
        corr[:, :, MARGIN + rows :, :] = jnp.zeros((images, lanes + 1, MARGIN, TILE), F32)
        hat[:, :, ABOVE + rows :, :] = jnp.zeros((images, lanes + 2, BELOW, TILE), BF16)

    @pl.when(jnp.logical_not(has_left))
    def _():
        halo_r[...] = jnp.zeros(halo_r.shape, F32)
        hat[:, 0, :, :] = jnp.zeros((images, ABOVE + rows + BELOW, TILE), BF16)

    @pl.when(jnp.logical_not(has_right))
    def _():
        halo_l[...] = jnp.zeros(halo_l.shape, F32)
        hat[:, lanes + 1, :, :] = jnp.zeros((images, ABOVE + rows + BELOW, TILE), BF16)

    def one(flag):
        return jnp.where(flag, 1, 0)

    expected = one(has_up) + one(has_down) + one(has_left) + one(has_right)
    expected += jnp.where(yy == 0, jnp.where(xx == 0, nx - 1, 1) + ny - 1, 1)
    pl.semaphore_wait(barrier, expected)

    def remote(source, target, send, recv, device):
        return pltpu.make_async_remote_copy(
            src_ref=source, dst_ref=target, send_sem=send, recv_sem=recv, device_id=device, device_id_type=MESH
        )

    def edge_rows(i):
        blocks = pl.ds(0, lanes)
        return (
            (has_down, has_up, remote(
                corr.at[i, blocks, pl.ds(rows, MARGIN)], corr.at[i, blocks, pl.ds(0, MARGIN)],
                p_send.at[i, 0], p_recv.at[i, 0], down)),
            (has_up, has_down, remote(
                corr.at[i, blocks, pl.ds(MARGIN, MARGIN)], corr.at[i, blocks, pl.ds(MARGIN + rows, MARGIN)],
                p_send.at[i, 1], p_recv.at[i, 1], up)),
        )

    def start(moves):
        for sends, _, copy in moves:
            pl.when(sends)(copy.start)

    def received(moves):
        for _, receives, copy in moves:
            pl.when(receives)(copy.wait_recv)

    def sent(moves):
        for sends, _, copy in moves:
            pl.when(sends)(copy.wait_send)

    def correct(k, carry):
        for copy in in_copies(k):
            copy.wait()

        def block(b, carry):
            at = pl.ds(pl.multiple_of(b * 16, 16), 16)
            to = pl.ds(pl.multiple_of(b * 16 + MARGIN, 8), 16)
            gain = 1.0 / flatv[k, at, :]
            offset = darkv[k, at, :]
            for c in range(images // channels):
                value = (rawv[c, k, at, :].astype(F32) - offset) * gain
                for t in range(lanes):
                    corr[c * channels + k, t, to, :] = value[:, t * TILE : (t + 1) * TILE]
            return carry

        lax.fori_loop(0, rows // 16, block, 0)
        for c in range(images // channels):
            start(edge_rows(c * channels + k))
        return carry

    lax.fori_loop(0, channels, correct, 0)

    tile_rows, tile_cols = rows // TILE, cols // TILE
    tiles = tile_rows * tile_cols
    source = lax.broadcasted_iota(jnp.int32, (3 * TILE, TILE), 0)
    target = lax.broadcasted_iota(jnp.int32, (3 * TILE, TILE), 1)
    apart = (source - target).astype(F32)

    def weigh(n, carry):
        c, rest = n // tiles, n % tiles
        i, j = rest // tile_cols, rest % tile_cols
        place = (shifts[c, i, j, 1] + TILE).astype(F32) + fractions[c, i, j, 1].astype(F32) / 8.0
        weights[n] = jnp.maximum(1.0 - jnp.abs(apart - place), 0.0).astype(BF16)
        return carry

    lax.fori_loop(0, (images // channels) * tiles, weigh, 0)

    def arrived(i, carry):
        received(edge_rows(i))
        return carry

    lax.fori_loop(0, images, arrived, 0)
    high = rows + 2 * MARGIN

    def pack(b, carry):
        at = pl.ds(pl.multiple_of(b * 8, 8), 8)
        lane = lane_iota(8)
        first = jnp.zeros((8, TILE), F32)
        last = jnp.zeros((8, TILE), F32)
        for i in range(images):
            low = pltpu.roll(corr[i, 0, at, :], MARGIN * i, 1)
            first = jnp.where((lane >= MARGIN * i) & (lane < MARGIN * (i + 1)), low, first)
            top = pltpu.roll(corr[i, lanes - 1, at, :], (72 + MARGIN * i) % TILE, 1)
            spot = 64 + MARGIN * i
            last = jnp.where((lane >= spot) & (lane < spot + MARGIN), top, last)
        pack_l[at, :] = first
        pack_r[at, :] = last
        return carry

    lax.fori_loop(0, high // 8, pack, 0)
    edge_cols = (
        (has_left, has_right, remote(pack_l, halo_l, c_send.at[0], c_recv.at[0], left)),
        (has_right, has_left, remote(pack_r, halo_r, c_send.at[1], c_recv.at[1], right)),
    )
    start(edge_cols)
    received(edge_cols)

    lo = MARGIN

    def hat_rows(i):
        blocks = pl.ds(1, lanes)
        return (
            (has_down, has_up, remote(
                hat.at[i, blocks, pl.ds(rows, ABOVE)], hat.at[i, blocks, pl.ds(0, ABOVE)],
                r_send.at[i, 0], r_recv.at[i, 0], down)),
            (has_up, has_down, remote(
                hat.at[i, blocks, pl.ds(ABOVE, BELOW)], hat.at[i, blocks, pl.ds(ABOVE + rows, BELOW)],
                r_send.at[i, 1], r_recv.at[i, 1], up)),
        )

    def hat_cols(i, part):
        at = pl.ds((ABOVE, 0, ABOVE + rows)[part], (rows, ABOVE, BELOW)[part])
        return (
            (has_left, has_right, remote(
                hat.at[i, 1, at], hat.at[i, lanes + 1, at], h_send.at[i, part, 0], h_recv.at[i, part, 0], left)),
            (has_right, has_left, remote(
                hat.at[i, lanes, at], hat.at[i, 0, at], h_send.at[i, part, 1], h_recv.at[i, part, 1], right)),
        )

    def tophat(i):
        turn_l = lax.rem(TILE - MARGIN * i, TILE)
        turn_r = 56 - MARGIN * i

        def erode_cols(b, carry):
            at = pl.ds(pl.multiple_of(b * 16, 16), 16)
            to = pl.ds(pl.multiple_of(b * 16 + lo, 8), 16)
            sides = jnp.where(
                lane_iota(16) < 64, pltpu.roll(halo_l[at, :], turn_l, 1), pltpu.roll(halo_r[at, :], turn_r, 1)
            )
            now = [corr[i, t, at, :] for t in range(lanes)] + [sides]
            for t, value in enumerate(lane_window(now, jnp.minimum, lanes + 1)):
                tmp1[t, to, :] = value
            return carry

        lax.fori_loop(0, high // 16, erode_cols, 0)

        def row_three(combine, count):
            def block(b, carry):
                base = b * 16 + lo
                for t in range(count):
                    value = combine(
                        combine(tmp1[t, pl.ds(base - 1, 16), :], tmp1[t, pl.ds(base, 16), :]),
                        tmp1[t, pl.ds(base + 1, 16), :],
                    )
                    tmp2[t, pl.ds(base, 16), :] = value
                return carry

            lax.fori_loop(0, high // 16, block, 0)

        def row_nine(combine, t, base):
            return combine(
                combine(tmp2[t, pl.ds(base - 3, 16), :], tmp2[t, pl.ds(base, 16), :]), tmp2[t, pl.ds(base + 3, 16), :]
            )

        row_three(jnp.minimum, lanes + 1)

        def erode_rows(b, carry):
            base = b * 16 + lo
            now = [row_nine(jnp.minimum, t, base) for t in range(lanes + 1)]
            for t, value in enumerate(lane_window(now, jnp.maximum, lanes)):
                tmp1[t, pl.ds(base, 16), :] = value
            return carry

        lax.fori_loop(0, high // 16, erode_rows, 0)
        row_three(jnp.maximum, lanes)

        def subtract(b, carry):
            base = b * 16 + MARGIN
            to = pl.ds(pl.multiple_of(b * 16 + ABOVE, 16), 16)
            for t in range(lanes):
                value = corr[i, t, pl.ds(base, 16), :] - row_nine(jnp.maximum, t, base + lo)
                hat[i, t + 1, to, :] = value.astype(BF16)
            return carry

        lax.fori_loop(0, rows // 16, subtract, 0)
        start(hat_rows(i))
        start(hat_cols(i, 0))

    def corners(i):
        received(hat_rows(i))
        for part in (1, 2):
            start(hat_cols(i, part))

    def out_copy(i):
        return pltpu.make_async_copy(reg.at[i], out.at[i // channels, i % channels], out_sem.at[i])

    def resample(i):
        for part in range(3):
            received(hat_cols(i, part))
        c = i // channels
        span = TILE + ABOVE + BELOW
        for n in range(tiles):
            ti, tj = n // tile_cols, n % tile_cols
            window = pl.ds(ti * TILE, span)
            near = jnp.concatenate([hat[i, tj + t, window, :] for t in range(3)], axis=1)
            moved = jnp.dot(near, weights[c * tiles + n], preferred_element_type=F32)
            mixed[n] = pltpu.roll(moved, (span - ABOVE) - shifts[c, ti, tj, 0], 0)
            lower = fractions[c, ti, tj, 0].astype(F32) / 8.0
            value = mixed[n, 0:TILE, :] * (1.0 - lower) + mixed[n, 1 : TILE + 1, :] * lower
            reg[i, ti * TILE : (ti + 1) * TILE, tj * TILE : (tj + 1) * TILE] = value.astype(BF16)
        out_copy(i).start()

    def panel_copy(device, slot):
        return remote(panel, panel, b_send.at[slot], b_recv.at[0], {"cyc": device})

    def ordered(j):
        return lax.rem(j, 2) * channels + lax.div(j, 2)

    def to_columns(act):
        for k in range(1, ny):
            act(panel_copy(k * nx + xx, nx + k))

    def to_row(act):
        for k in range(1, nx):
            act(panel_copy(k, k))

    def begin(copy):
        copy.start()

    def end(copy):
        copy.wait_send()

    def step(s, carry):
        @pl.when(s < images)
        def _():
            tophat(ordered(s))

        @pl.when((s >= LAG) & (s < LAG + images))
        def _():
            corners(ordered(s - LAG))

        @pl.when(s >= LAG + 1)
        def _():
            resample(ordered(s - LAG - 1))

        @pl.when((s == LAG + 1) & (cyc == 0))
        def _():
            panel[...] = reg[0]
            to_row(begin)
            to_columns(begin)

        @pl.when((s == LAG + 5) & (yy == 0) & (xx > 0))
        def _():
            panel_copy(0, 0).wait_recv()
            to_columns(begin)

        return carry

    lax.fori_loop(0, images + LAG + 1, step, 0)

    @pl.when(yy > 0)
    def _():
        panel_copy(0, 0).wait_recv()

    box_rows, box_cols = rows // BOX, cols // BOX
    gather = (lax.broadcasted_iota(jnp.int32, (cols, box_cols), 0) // BOX
              == lax.broadcasted_iota(jnp.int32, (cols, box_cols), 1)).astype(F32)
    spread = (lax.broadcasted_iota(jnp.int32, (box_cols, cols), 1) // BOX
              == lax.broadcasted_iota(jnp.int32, (box_cols, cols), 0)).astype(F32)
    exact = functools.partial(jnp.dot, precision=lax.Precision.HIGHEST, preferred_element_type=F32)
    area = 1.0 / (BOX * BOX)

    def stains(b):
        at = pl.ds(b * BOX, BOX)
        return [reg[c * channels, at, :].astype(F32) for c in range(images // channels)] + [panel[at, :].astype(F32)]

    for b in range(box_rows):
        for n, value in enumerate(stains(b)):
            sums[n, pl.ds(b, 1), :] = jnp.sum(value, axis=0, keepdims=True)
    cycles = images // channels
    for n in range(cycles + 1):
        means[n] = exact(exact(sums[n], gather) * area, spread)
    for b in range(box_rows):
        centred = [value - means[n, pl.ds(b, 1), :] for n, value in enumerate(stains(b))]
        fixed = centred[cycles]
        terms = [value * fixed for value in centred] + [value * value for value in centred[:cycles]]
        for n, value in enumerate(terms):
            sums[n, pl.ds(b, 1), :] = jnp.sum(value, axis=0, keepdims=True)
    fixed_var = exact(sums[cycles], gather) * area
    for c in range(cycles):
        covar = exact(sums[c], gather) * area
        var = exact(sums[cycles + 1 + c], gather) * area
        scores[c] = covar / jnp.sqrt(var * fixed_var + 1e-06)

    def finish(i, carry):
        sent(edge_rows(i))
        sent(hat_rows(i))
        for part in range(3):
            sent(hat_cols(i, part))
        out_copy(i).wait()
        return carry

    lax.fori_loop(0, images, finish, 0)
    sent(edge_cols)

    @pl.when(cyc == 0)
    def _():
        to_row(end)

    @pl.when(yy == 0)
    def _():
        to_columns(end)


def body(sizes, raw, flat, dark, shifts, fractions):
    cycles, channels, rows, cols = raw.shape
    images, lanes = cycles * channels, cols // TILE
    tiles = (rows // TILE) * lanes
    high = rows + 2 * MARGIN
    dma = pltpu.SemaphoreType.DMA
    anywhere = pl.BlockSpec(memory_space=pl.ANY)
    scalars = pl.BlockSpec(memory_space=pltpu.SMEM)
    vmem = pl.BlockSpec(memory_space=pltpu.VMEM)
    nx = math.isqrt(sizes[0])
    registered, scores = pl.pallas_call(
        functools.partial(kernel, sizes + (nx,)),
        out_shape=(
            jax.ShapeDtypeStruct(raw.shape, BF16),
            jax.ShapeDtypeStruct((cycles, rows // BOX, cols // BOX), F32),
        ),
        in_specs=[anywhere, anywhere, anywhere, scalars, scalars],
        out_specs=(anywhere, vmem),
        scratch_shapes=[
            pltpu.VMEM(raw.shape, BF16),
            pltpu.VMEM(flat.shape, F32),
            pltpu.VMEM(dark.shape, F32),
            pltpu.VMEM((images, lanes + 1, high, TILE), F32),
            pltpu.VMEM((high, TILE), F32),
            pltpu.VMEM((high, TILE), F32),
            pltpu.VMEM((high, TILE), F32),
            pltpu.VMEM((high, TILE), F32),
            pltpu.VMEM((lanes + 1, high + 2 * MARGIN, TILE), F32),
            pltpu.VMEM((lanes + 1, high + 2 * MARGIN, TILE), F32),
            pltpu.VMEM((images, lanes + 2, ABOVE + rows + BELOW, TILE), BF16),
            pltpu.VMEM((tiles, TILE + ABOVE + BELOW, TILE), F32),
            pltpu.VMEM((cycles * tiles, 3 * TILE, TILE), BF16),
            pltpu.VMEM((images, rows, cols), BF16),
            pltpu.VMEM((rows, cols), BF16),
            pltpu.VMEM((2 * cycles + 1, rows // BOX, cols), F32),
            pltpu.VMEM((cycles + 1, rows // BOX, cols), F32),
            dma((channels, 3)),
            dma((images,)),
            dma((images, 2)),
            dma((images, 2)),
            dma((2,)),
            dma((2,)),
            dma((images, 2)),
            dma((images, 2)),
            dma((images, 3, 2)),
            dma((images, 3, 2)),
            dma((nx + sizes[0] // nx,)),
            dma((1,)),
        ],
        compiler_params=pltpu.CompilerParams(
            collective_id=0, has_side_effects=True, vmem_limit_bytes=56 * 1024 * 1024
        ),
    )(raw, flat, dark, shifts, fractions)
    return registered, scores


def solution(mesh):
    sizes = (mesh.shape["cyc"], mesh.shape["row"], mesh.shape["col"])
    return jax.shard_map(
        functools.partial(body, sizes),
        mesh=mesh,
        in_specs=(
            P("cyc", None, "row", "col"),
            P(None, "row", "col"),
            P(None, "row", "col"),
            P("cyc", "row", "col", None),
            P("cyc", "row", "col", None),
        ),
        out_specs=(P("cyc", None, "row", "col"), P("cyc", "row", "col")),
        check_vma=False,
    )
```

time: 368 us -> 109 us (0.30)
  the two profiles are of different devices: /device:TPU:1 before, /device:TPU:54 now
where the time goes in v1:
time: 109 us
  Pallas kernels  102 us (94%)
  local copies, waits for them, and re-layouts  6.42 us (6%)
    pallas_call x1, Pallas kernels, body(): pl.pallas_call(functools.partial(kernel, sizes + (nx,)), out_shape=(jax.S...  102 us
    unnamed x6, local copies, waits for them, and re-layouts  6.42 us

profile of v1, /device:TPU:54, one launch (start us, length us, event | category | flops | bytes accessed | tf_op | source)
XLA Modules:
  0.0 108.7 jit_solution(6990677345385066167)
XLA Ops:
  0.6 1.4 %copy.7.shifts = s32[2,2,4,2]{3,2,1,0:T(4,128)} copy(s32[2,2,4,2]{2,3,1,0:T(2,128)} %param.8) | data formatting | bytes 256 | tf_op args[3]
  2.0 1.4 %copy.8.fractions = s32[2,2,4,2]{3,2,1,0:T(4,128)} copy(s32[2,2,4,2]{2,3,1,0:T(2,128)} %param.9) | data formatting | bytes 256 | tf_op args[4]
  3.4 101.6 %shard_map.68 = (bf16[2,4,256,512]{3,2,1,0:T(8,128)(2,1)}, f32[2,8,16]{2,1,0:T(8,128)}) custom-call(bf16[2,4,256,512]{3,2,1,0:T(8,128)(2,1)} %raw.1, f32[4,256,512]{2,1,0:T(8,128)} %flat.1, f32[4,256,512]{2,1,0:T(8,128)} %dark.1, s32[2,2,4,2]{3,2,1,0:T(4,128)} %copy.7.shifts, s32[2,2,4,2]{3,2,1,0:T(4,128)} %copy.8.fractions), custom_call_target="tpu_custom_call" | custom-call | tf_op jit(solution)/shard_map/pallas_call | solution.py:424
  105.0 0.0 copy-start
  105.0 3.0 %copy.11 = bf16[2,4,256,512]{3,2,1,0:T(8,128)(2,1)} copy(bf16[2,4,256,512]{3,2,1,0:T(8,128)(2,1)} %get-tuple-element.4) | data formatting | bytes 4194304
  108.1 0.0 copy-done
  108.1 0.6 copy.12
Async XLA Ops:
  105.0 3.1 %copy-start = (f32[2,8,16]{2,1,0:T(8,128)S(1)}, f32[2,8,16]{2,1,0:T(8,128)}, u32[]{:S(2)}) copy-start(f32[2,8,16]{2,1,0:T(8,128)} %get-tuple-element.5) | copy-start | bytes 3076

commit v2 on v1

--- a/solution.py
+++ b/solution.py
@@ -12,6 +12,8 @@
 MARGIN = 8
 ABOVE = 48
 BELOW = 64
+EDGE = 16
+CHUNK = 136
 BOX = 32
 LAG = 3
 MESH = pl.DeviceIdType.MESH
@@ -19,31 +21,23 @@
 BF16 = jnp.bfloat16
 
 
-def lane_iota(rows):
-    return lax.broadcasted_iota(jnp.int32, (rows, TILE), 1)
-
-
-def shifted(tiles, step):
-    count = len(tiles)
-    rolled = [pltpu.roll(tile, (-step) % TILE, 1) for tile in tiles]
-    lane = lane_iota(tiles[0].shape[0])
-    if step > 0:
-        return [jnp.where(lane < TILE - step, rolled[t], rolled[(t + 1) % count]) for t in range(count)]
-    return [jnp.where(lane >= -step, rolled[t], rolled[(t - 1) % count]) for t in range(count)]
-
-
-def lane_window(tiles, combine, outputs):
-    ahead, behind = shifted(tiles, 1), shifted(tiles, -1)
-    three = [combine(combine(a, b), c) for a, b, c in zip(tiles, ahead, behind)]
-    ahead, behind = shifted(three, 3), shifted(three, -3)
-    return [combine(combine(three[t], ahead[t]), behind[t]) for t in range(outputs)]
+def spread_three(source, target, combine, start, count):
+    for at in range(start, start + count, CHUNK):
+        size = min(CHUNK, start + count - at)
+        near = combine(source[pl.ds(at - 1, size), :], source[pl.ds(at, size), :])
+        target[pl.ds(at, size), :] = combine(near, source[pl.ds(at + 1, size), :])
+
+
+def spread_nine(source, combine, at, size):
+    near = combine(source[pl.ds(at - 3, size), :], source[pl.ds(at, size), :])
+    return combine(near, source[pl.ds(at + 3, size), :])
 
 
 def kernel(
     sizes, raw, flat, dark, shifts, fractions, out, scores,
-    rawv, flatv, darkv, corr, pack_l, pack_r, halo_l, halo_r, tmp1, tmp2, hat, mixed, weights, reg, panel,
+    rawv, flatv, darkv, corr, tall, brims, brims_back, wide1, wide2, three, back, hat, next_s, next_r, mixed, weights, reg, panel,
     sums, means,
-    in_sem, out_sem, p_send, p_recv, c_send, c_recv, r_send, r_recv, h_send, h_recv, b_send, b_recv,
+    in_sem, out_sem, p_send, p_recv, c_send, c_recv, r_send, r_recv, n_send, n_recv, h_send, h_recv, b_send, b_recv,
 ):
     n_cyc, n_row, n_col, nx = sizes
     ny = n_cyc // nx
@@ -82,24 +76,26 @@
         pl.when(yy == 0)(functools.partial(greet, {"cyc": k * nx + xx}))
     pl.when(yy > 0)(functools.partial(greet, {"cyc": xx}))
 
+    next_s[...] = jnp.zeros(next_s.shape, F32)
+
     @pl.when(jnp.logical_not(has_up))
     def _():
-        corr[:, :, 0:MARGIN, :] = jnp.zeros((images, lanes + 1, MARGIN, TILE), F32)
+        corr[:, :, MARGIN:EDGE, :] = jnp.zeros((images, lanes, MARGIN, TILE), F32)
         hat[:, :, 0:ABOVE, :] = jnp.zeros((images, lanes + 2, ABOVE, TILE), BF16)
 
     @pl.when(jnp.logical_not(has_down))
     def _():
-        corr[:, :, MARGIN + rows :, :] = jnp.zeros((images, lanes + 1, MARGIN, TILE), F32)
+        corr[:, :, EDGE + rows : EDGE + rows + MARGIN, :] = jnp.zeros((images, lanes, MARGIN, TILE), F32)
         hat[:, :, ABOVE + rows :, :] = jnp.zeros((images, lanes + 2, BELOW, TILE), BF16)
 
     @pl.when(jnp.logical_not(has_left))
     def _():
-        halo_r[...] = jnp.zeros(halo_r.shape, F32)
+        tall[:, MARGIN:EDGE, :] = jnp.zeros((2 * images + 1, MARGIN, TILE), F32)
         hat[:, 0, :, :] = jnp.zeros((images, ABOVE + rows + BELOW, TILE), BF16)
 
     @pl.when(jnp.logical_not(has_right))
     def _():
-        halo_l[...] = jnp.zeros(halo_l.shape, F32)
+        tall[:, EDGE + cols : EDGE + cols + MARGIN, :] = jnp.zeros((2 * images + 1, MARGIN, TILE), F32)
         hat[:, lanes + 1, :, :] = jnp.zeros((images, ABOVE + rows + BELOW, TILE), BF16)
 
     def one(flag):
@@ -115,13 +111,12 @@
         )
 
     def edge_rows(i):
-        blocks = pl.ds(0, lanes)
         return (
             (has_down, has_up, remote(
-                corr.at[i, blocks, pl.ds(rows, MARGIN)], corr.at[i, blocks, pl.ds(0, MARGIN)],
+                corr.at[i, :, pl.ds(rows + MARGIN, MARGIN)], corr.at[i, :, pl.ds(MARGIN, MARGIN)],
                 p_send.at[i, 0], p_recv.at[i, 0], down)),
             (has_up, has_down, remote(
-                corr.at[i, blocks, pl.ds(MARGIN, MARGIN)], corr.at[i, blocks, pl.ds(MARGIN + rows, MARGIN)],
+                corr.at[i, :, pl.ds(EDGE, MARGIN)], corr.at[i, :, pl.ds(EDGE + rows, MARGIN)],
                 p_send.at[i, 1], p_recv.at[i, 1], up)),
         )
 
@@ -143,7 +138,7 @@
 
         def block(b, carry):
             at = pl.ds(pl.multiple_of(b * 16, 16), 16)
-            to = pl.ds(pl.multiple_of(b * 16 + MARGIN, 8), 16)
+            to = pl.ds(pl.multiple_of(b * 16 + EDGE, 16), 16)
             gain = 1.0 / flatv[k, at, :]
             offset = darkv[k, at, :]
             for c in range(images // channels):
@@ -174,37 +169,50 @@
 
     lax.fori_loop(0, (images // channels) * tiles, weigh, 0)
 
-    def arrived(i, carry):
+    halves = rows // TILE
+    brims[:, images * MARGIN :, :] = jnp.zeros((lanes, TILE - images * MARGIN, TILE), F32)
+    upper = lax.broadcasted_iota(jnp.int32, (MARGIN, TILE), 0) >= MARGIN // 2
+
+    def erode(i, carry):
         received(edge_rows(i))
+        for t in range(lanes):
+            spread_three(corr.at[i, t], three.at[t], jnp.minimum, MARGIN, rows + 2 * MARGIN)
+        for t in range(lanes):
+            for b in range(halves):
+                value = spread_nine(three.at[t], jnp.minimum, EDGE + b * TILE, TILE)
+                tall[halves * i + b, EDGE + t * TILE : EDGE + (t + 1) * TILE, :] = value.T
+            above = spread_nine(three.at[t], jnp.minimum, MARGIN, MARGIN)
+            below = spread_nine(three.at[t], jnp.minimum, EDGE + rows, MARGIN)
+            brims[t, pl.ds(pl.multiple_of(MARGIN * i, MARGIN), MARGIN), :] = jnp.where(upper, above, below)
         return carry
 
-    lax.fori_loop(0, images, arrived, 0)
-    high = rows + 2 * MARGIN
-
-    def pack(b, carry):
-        at = pl.ds(pl.multiple_of(b * 8, 8), 8)
-        lane = lane_iota(8)
-        first = jnp.zeros((8, TILE), F32)
-        last = jnp.zeros((8, TILE), F32)
-        for i in range(images):
-            low = pltpu.roll(corr[i, 0, at, :], MARGIN * i, 1)
-            first = jnp.where((lane >= MARGIN * i) & (lane < MARGIN * (i + 1)), low, first)
-            top = pltpu.roll(corr[i, lanes - 1, at, :], (72 + MARGIN * i) % TILE, 1)
-            spot = 64 + MARGIN * i
-            last = jnp.where((lane >= spot) & (lane < spot + MARGIN), top, last)
-        pack_l[at, :] = first
-        pack_r[at, :] = last
-        return carry
-
-    lax.fori_loop(0, high // 8, pack, 0)
+    lax.fori_loop(0, images, erode, 0)
+    for t in range(lanes):
+        tall[halves * images, EDGE + t * TILE : EDGE + (t + 1) * TILE, :] = brims[t].T
     edge_cols = (
-        (has_left, has_right, remote(pack_l, halo_l, c_send.at[0], c_recv.at[0], left)),
-        (has_right, has_left, remote(pack_r, halo_r, c_send.at[1], c_recv.at[1], right)),
+        (has_left, has_right, remote(
+            tall.at[:, pl.ds(EDGE, MARGIN)], tall.at[:, pl.ds(EDGE + cols, MARGIN)],
+            c_send.at[0], c_recv.at[0], left)),
+        (has_right, has_left, remote(
+            tall.at[:, pl.ds(cols + MARGIN, MARGIN)], tall.at[:, pl.ds(MARGIN, MARGIN)],
+            c_send.at[1], c_recv.at[1], right)),
     )
     start(edge_cols)
     received(edge_cols)
 
-    lo = MARGIN
+    def across(n, place):
+        spread_three(tall.at[n], wide1, jnp.minimum, MARGIN, cols + 2 * MARGIN)
+        for at in range(MARGIN, cols + EDGE + MARGIN, CHUNK):
+            size = min(CHUNK, cols + EDGE + MARGIN - at)
+            wide2[at : at + size, :] = spread_nine(wide1, jnp.minimum, at, size)
+        spread_three(wide2, wide1, jnp.maximum, MARGIN, cols + 2 * MARGIN)
+        for t in range(lanes):
+            place(t, spread_nine(wide1, jnp.maximum, EDGE + t * TILE, TILE).T)
+
+    def keep_brims(t, value):
+        brims_back[t] = value
+
+    across(halves * images, keep_brims)
 
     def hat_rows(i):
         blocks = pl.ds(1, lanes)
@@ -213,8 +221,9 @@
                 hat.at[i, blocks, pl.ds(rows, ABOVE)], hat.at[i, blocks, pl.ds(0, ABOVE)],
                 r_send.at[i, 0], r_recv.at[i, 0], down)),
             (has_up, has_down, remote(
-                hat.at[i, blocks, pl.ds(ABOVE, BELOW)], hat.at[i, blocks, pl.ds(ABOVE + rows, BELOW)],
+                hat.at[i, blocks, pl.ds(ABOVE, ABOVE)], hat.at[i, blocks, pl.ds(ABOVE + rows, ABOVE)],
                 r_send.at[i, 1], r_recv.at[i, 1], up)),
+            (has_up, has_down, remote(next_s.at[i], next_r.at[i], n_send.at[i], n_recv.at[i], up)),
         )
 
     def hat_cols(i, part):
@@ -227,66 +236,37 @@
         )
 
     def tophat(i):
-        turn_l = lax.rem(TILE - MARGIN * i, TILE)
-        turn_r = 56 - MARGIN * i
-
-        def erode_cols(b, carry):
-            at = pl.ds(pl.multiple_of(b * 16, 16), 16)
-            to = pl.ds(pl.multiple_of(b * 16 + lo, 8), 16)
-            sides = jnp.where(
-                lane_iota(16) < 64, pltpu.roll(halo_l[at, :], turn_l, 1), pltpu.roll(halo_r[at, :], turn_r, 1)
-            )
-            now = [corr[i, t, at, :] for t in range(lanes)] + [sides]
-            for t, value in enumerate(lane_window(now, jnp.minimum, lanes + 1)):
-                tmp1[t, to, :] = value
-            return carry
-
-        lax.fori_loop(0, high // 16, erode_cols, 0)
-
-        def row_three(combine, count):
-            def block(b, carry):
-                base = b * 16 + lo
-                for t in range(count):
-                    value = combine(
-                        combine(tmp1[t, pl.ds(base - 1, 16), :], tmp1[t, pl.ds(base, 16), :]),
-                        tmp1[t, pl.ds(base + 1, 16), :],
-                    )
-                    tmp2[t, pl.ds(base, 16), :] = value
-                return carry
-
-            lax.fori_loop(0, high // 16, block, 0)
-
-        def row_nine(combine, t, base):
-            return combine(
-                combine(tmp2[t, pl.ds(base - 3, 16), :], tmp2[t, pl.ds(base, 16), :]), tmp2[t, pl.ds(base + 3, 16), :]
-            )
-
-        row_three(jnp.minimum, lanes + 1)
-
-        def erode_rows(b, carry):
-            base = b * 16 + lo
-            now = [row_nine(jnp.minimum, t, base) for t in range(lanes + 1)]
-            for t, value in enumerate(lane_window(now, jnp.maximum, lanes)):
-                tmp1[t, pl.ds(base, 16), :] = value
-            return carry
-
-        lax.fori_loop(0, high // 16, erode_rows, 0)
-        row_three(jnp.maximum, lanes)
-
-        def subtract(b, carry):
-            base = b * 16 + MARGIN
-            to = pl.ds(pl.multiple_of(b * 16 + ABOVE, 16), 16)
-            for t in range(lanes):
-                value = corr[i, t, pl.ds(base, 16), :] - row_nine(jnp.maximum, t, base + lo)
-                hat[i, t + 1, to, :] = value.astype(BF16)
-            return carry
-
-        lax.fori_loop(0, rows // 16, subtract, 0)
+        for b in range(halves):
+            def keep(t, value, b=b):
+                back[t, EDGE + b * TILE : EDGE + (b + 1) * TILE, :] = value
+
+            across(halves * i + b, keep)
+        for t in range(lanes):
+            ends = brims_back[t, pl.ds(pl.multiple_of(MARGIN * i, MARGIN), MARGIN), :]
+            back[t, MARGIN:EDGE, :] = ends
+            back[t, EDGE + rows : EDGE + rows + MARGIN, :] = ends
+        for t in range(lanes):
+            spread_three(back.at[t], three.at[t], jnp.maximum, MARGIN, rows + 2 * MARGIN)
+        for t in range(lanes):
+            for b in range(halves):
+                opened = spread_nine(three.at[t], jnp.maximum, EDGE + b * TILE, TILE)
+                value = (corr[i, t, EDGE + b * TILE : EDGE + (b + 1) * TILE, :] - opened).astype(BF16)
+                hat[i, t + 1, ABOVE + b * TILE : ABOVE + (b + 1) * TILE, :] = value
+                if b == 0:
+                    next_s[i, t : t + 1, :] = value[ABOVE : ABOVE + 16].astype(F32)[0:1]
         start(hat_rows(i))
         start(hat_cols(i, 0))
 
     def corners(i):
         received(hat_rows(i))
+
+        @pl.when(has_down)
+        def _():
+            first = lax.broadcasted_iota(jnp.int32, (16, TILE), 0) == 0
+            for t in range(lanes):
+                value = jnp.where(first, next_r[i, t : t + 1, :], 0.0)
+                hat[i, t + 1, ABOVE + rows + ABOVE :, :] = value.astype(BF16)
+
         for part in (1, 2):
             start(hat_cols(i, part))
 
@@ -415,7 +395,6 @@
     cycles, channels, rows, cols = raw.shape
     images, lanes = cycles * channels, cols // TILE
     tiles = (rows // TILE) * lanes
-    high = rows + 2 * MARGIN
     dma = pltpu.SemaphoreType.DMA
     anywhere = pl.BlockSpec(memory_space=pl.ANY)
     scalars = pl.BlockSpec(memory_space=pltpu.SMEM)
@@ -433,14 +412,17 @@
             pltpu.VMEM(raw.shape, BF16),
             pltpu.VMEM(flat.shape, F32),
             pltpu.VMEM(dark.shape, F32),
-            pltpu.VMEM((images, lanes + 1, high, TILE), F32),
-            pltpu.VMEM((high, TILE), F32),
-            pltpu.VMEM((high, TILE), F32),
-            pltpu.VMEM((high, TILE), F32),
-            pltpu.VMEM((high, TILE), F32),
-            pltpu.VMEM((lanes + 1, high + 2 * MARGIN, TILE), F32),
-            pltpu.VMEM((lanes + 1, high + 2 * MARGIN, TILE), F32),
+            pltpu.VMEM((images, lanes, rows + 2 * EDGE, TILE), F32),
+            pltpu.VMEM((images * (rows // TILE) + 1, cols + 2 * EDGE, TILE), F32),
+            pltpu.VMEM((lanes, TILE, TILE), F32),
+            pltpu.VMEM((lanes, TILE, TILE), F32),
+            pltpu.VMEM((cols + 2 * EDGE, TILE), F32),
+            pltpu.VMEM((cols + 2 * EDGE, TILE), F32),
+            pltpu.VMEM((lanes, rows + 2 * EDGE, TILE), F32),
+            pltpu.VMEM((lanes, rows + 2 * EDGE, TILE), F32),
             pltpu.VMEM((images, lanes + 2, ABOVE + rows + BELOW, TILE), BF16),
+            pltpu.VMEM((images, 8, TILE), F32),
+            pltpu.VMEM((images, 8, TILE), F32),
             pltpu.VMEM((tiles, TILE + ABOVE + BELOW, TILE), F32),
             pltpu.VMEM((cycles * tiles, 3 * TILE, TILE), BF16),
             pltpu.VMEM((images, rows, cols), BF16),
@@ -455,6 +437,8 @@
             dma((2,)),
             dma((images, 2)),
             dma((images, 2)),
+            dma((images,)),
+            dma((images,)),
             dma((images, 3, 2)),
             dma((images, 3, 2)),
             dma((nx + sizes[0] // nx,)),

time: 109 us -> 66.8 us (0.61)
  the two profiles are of different devices: /device:TPU:54 before, /device:TPU:114 now
where the time goes in v2:
time: 66.8 us; the launch traced here: 66.6 us
  Pallas kernels  59.5 us (89%)
  local copies, waits for them, and re-layouts  6.42 us (10%)
    pallas_call x1, Pallas kernels, body(): pl.pallas_call(functools.partial(kernel, sizes + (nx,)), out_shape=(jax.S...  59.5 us
    unnamed x6, local copies, waits for them, and re-layouts  6.42 us

profile of v2, /device:TPU:114, one launch (start us, length us, event | category | flops | bytes accessed | tf_op | source)
XLA Modules:
  0.0 66.6 jit_solution(18130719197283387452)
XLA Ops:
  0.6 1.4 %copy.7.shifts = s32[2,2,4,2]{3,2,1,0:T(4,128)} copy(s32[2,2,4,2]{2,3,1,0:T(2,128)} %param.8) | data formatting | bytes 256 | tf_op args[3]
  2.0 1.4 %copy.8.fractions = s32[2,2,4,2]{3,2,1,0:T(4,128)} copy(s32[2,2,4,2]{2,3,1,0:T(2,128)} %param.9) | data formatting | bytes 256 | tf_op args[4]
  3.4 59.5 %shard_map.68 = (bf16[2,4,256,512]{3,2,1,0:T(8,128)(2,1)}, f32[2,8,16]{2,1,0:T(8,128)}) custom-call(bf16[2,4,256,512]{3,2,1,0:T(8,128)(2,1)} %raw.1, f32[4,256,512]{2,1,0:T(8,128)} %flat.1, f32[4,256,512]{2,1,0:T(8,128)} %dark.1, s32[2,2,4,2]{3,2,1,0:T(4,128)} %copy.7.shifts, s32[2,2,4,2]{3,2,1,0:T(4,128)} %copy.8.fractions), custom_call_target="tpu_custom_call" | custom-call | tf_op jit(solution)/shard_map/pallas_call | solution.py:403
  62.9 0.0 copy-start
  62.9 3.0 %copy.11 = bf16[2,4,256,512]{3,2,1,0:T(8,128)(2,1)} copy(bf16[2,4,256,512]{3,2,1,0:T(8,128)(2,1)} %get-tuple-element.4) | data formatting | bytes 4194304
  66.0 0.0 copy-done
  66.0 0.6 copy.12
Async XLA Ops:
  62.9 3.1 %copy-start = (f32[2,8,16]{2,1,0:T(8,128)S(1)}, f32[2,8,16]{2,1,0:T(8,128)}, u32[]{:S(2)}) copy-start(f32[2,8,16]{2,1,0:T(8,128)} %get-tuple-element.5) | copy-start | bytes 3076

commit v3 on v2

v3 whole, which is shorter than its diff:
```python
import functools
import math

import jax
import jax.numpy as jnp
from jax import lax
from jax.experimental import pallas as pl
from jax.experimental.pallas import tpu as pltpu
from jax.sharding import PartitionSpec as P

TILE = 128
MARGIN = 8
ABOVE = 48
BELOW = 64
EDGE = 16
CHUNK = 136
BOX = 32
LAG = 2
MESH = pl.DeviceIdType.MESH
F32 = jnp.float32
BF16 = jnp.bfloat16


def spread_three(source, target, combine, start, count):
    for at in range(start, start + count, CHUNK):
        size = min(CHUNK, start + count - at)
        near = combine(source[pl.ds(at - 1, size), :], source[pl.ds(at, size), :])
        target[pl.ds(at, size), :] = combine(near, source[pl.ds(at + 1, size), :])


def spread_nine(source, combine, at, size):
    near = combine(source[pl.ds(at - 3, size), :], source[pl.ds(at, size), :])
    return combine(near, source[pl.ds(at + 3, size), :])


def kernel(
    sizes, raw, flat, dark, shifts_in, fractions_in, out, scores, shifts, fractions,
    rawv, flatv, darkv, corr, tall, brims, brims_back, wide1, wide2, three, back, hat, next_s, next_r, side_s, side_r, corner_s, corner_r, mixed, weights, reg, panel,
    sums, means,
    in_sem, scalar_sem, out_sem, p_send, p_recv, c_send, c_recv, r_send, r_recv, n_send, n_recv, h_send, h_recv, b_send, b_recv,
):
    n_cyc, n_row, n_col, nx = sizes
    ny = n_cyc // nx
    channels, rows, cols = flat.shape
    cycles = raw.shape[0]
    images = cycles * channels
    halves = rows // TILE
    lanes = cols // TILE
    cyc, row, col = lax.axis_index("cyc"), lax.axis_index("row"), lax.axis_index("col")
    yy, xx = cyc // nx, cyc % nx
    has_up, has_down = row > 0, row < n_row - 1
    has_left, has_right = col > 0, col < n_col - 1
    up, down = {"row": row - 1}, {"row": row + 1}
    left, right = {"col": col - 1}, {"col": col + 1}

    def in_copies(k):
        return (
            pltpu.make_async_copy(raw.at[:, k], rawv.at[:, k], in_sem.at[k, 0]),
            pltpu.make_async_copy(flat.at[k], flatv.at[k], in_sem.at[k, 1]),
            pltpu.make_async_copy(dark.at[k], darkv.at[k], in_sem.at[k, 2]),
        )

    for k in range(channels):
        for copy in in_copies(k):
            copy.start()

    scalars = (
        pltpu.make_async_copy(shifts_in, shifts, scalar_sem.at[0]),
        pltpu.make_async_copy(fractions_in, fractions, scalar_sem.at[1]),
    )
    for copy in scalars:
        copy.start()

    barrier = pltpu.get_barrier_semaphore()

    def greet(device):
        pl.semaphore_signal(barrier, inc=1, device_id=device, device_id_type=MESH)

    for there, device in ((has_up, up), (has_down, down), (has_left, left), (has_right, right)):
        pl.when(there)(functools.partial(greet, device))
    for k in range(1, nx):
        greet({"cyc": yy * nx + lax.rem(xx + k, nx)})
    for k in range(1, ny):
        pl.when(yy == 0)(functools.partial(greet, {"cyc": k * nx + xx}))
    pl.when(yy > 0)(functools.partial(greet, {"cyc": xx}))

    next_s[...] = jnp.zeros(next_s.shape, F32)

    @pl.when(jnp.logical_not(has_up))
    def _():
        corr[:, :, MARGIN:EDGE, :] = jnp.zeros((images, lanes, MARGIN, TILE), F32)
        hat[:, :, 0:ABOVE, :] = jnp.zeros((images, lanes + 2, ABOVE, TILE), BF16)

    @pl.when(jnp.logical_not(has_down))
    def _():
        corr[:, :, EDGE + rows : EDGE + rows + MARGIN, :] = jnp.zeros((images, lanes, MARGIN, TILE), F32)
        hat[:, :, ABOVE + rows :, :] = jnp.zeros((images, lanes + 2, BELOW, TILE), BF16)

    @pl.when(jnp.logical_not(has_left))
    def _():
        tall[:, :, MARGIN:EDGE, :] = jnp.zeros((channels, halves * cycles + 1, MARGIN, TILE), F32)
        side_r[:, 1] = jnp.zeros((images, TILE, TILE), BF16)
        corner_r[:, 1] = jnp.zeros((images, BELOW, TILE), BF16)

    @pl.when(jnp.logical_not(has_right))
    def _():
        tall[:, :, EDGE + cols : EDGE + cols + MARGIN, :] = jnp.zeros((channels, halves * cycles + 1, MARGIN, TILE), F32)
        side_r[:, 0] = jnp.zeros((images, TILE, TILE), BF16)
        corner_r[:, 0] = jnp.zeros((images, BELOW, TILE), BF16)

    def one(flag):
        return jnp.where(flag, 1, 0)

    expected = one(has_up) + one(has_down) + one(has_left) + one(has_right)
    expected += nx - 1 + jnp.where(yy == 0, ny - 1, 1)
    pl.semaphore_wait(barrier, expected)

    def remote(source, target, send, recv, device):
        return pltpu.make_async_remote_copy(
            src_ref=source, dst_ref=target, send_sem=send, recv_sem=recv, device_id=device, device_id_type=MESH
        )

    def edge_rows(i):
        return (
            (has_down, has_up, remote(
                corr.at[i, :, pl.ds(rows + MARGIN, MARGIN)], corr.at[i, :, pl.ds(MARGIN, MARGIN)],
                p_send.at[i, 0], p_recv.at[i, 0], down)),
            (has_up, has_down, remote(
                corr.at[i, :, pl.ds(EDGE, MARGIN)], corr.at[i, :, pl.ds(EDGE + rows, MARGIN)],
                p_send.at[i, 1], p_recv.at[i, 1], up)),
        )

    def start(moves):
        for sends, _, copy in moves:
            pl.when(sends)(copy.start)

    def received(moves):
        for _, receives, copy in moves:
            pl.when(receives)(copy.wait_recv)

    def sent(moves):
        for sends, _, copy in moves:
            pl.when(sends)(copy.wait_send)

    def correct(k, carry):
        for copy in in_copies(k):
            copy.wait()

        def block(b, carry):
            at = pl.ds(pl.multiple_of(b * 16, 16), 16)
            to = pl.ds(pl.multiple_of(b * 16 + EDGE, 16), 16)
            gain = 1.0 / flatv[k, at, :]
            offset = darkv[k, at, :]
            for c in range(cycles):
                value = (rawv[c, k, at, :].astype(F32) - offset) * gain
                for t in range(lanes):
                    corr[c * channels + k, t, to, :] = value[:, t * TILE : (t + 1) * TILE]
            return carry

        lax.fori_loop(0, rows // 16, block, 0)
        for c in range(cycles):
            start(edge_rows(c * channels + k))
        return carry

    lax.fori_loop(0, channels, correct, 0)

    tile_rows, tile_cols = rows // TILE, cols // TILE
    tiles = tile_rows * tile_cols
    source = lax.broadcasted_iota(jnp.int32, (3 * TILE, TILE), 0)
    target = lax.broadcasted_iota(jnp.int32, (3 * TILE, TILE), 1)
    apart = (source - target).astype(F32)

    def weigh(n, carry):
        c, rest = n // tiles, n % tiles
        i, j = rest // tile_cols, rest % tile_cols
        place = (shifts[c, i, 1, j] + TILE).astype(F32) + fractions[c, i, 1, j].astype(F32) / 8.0
        weights[n] = jnp.maximum(1.0 - jnp.abs(apart - place), 0.0).astype(BF16)
        return carry

    for copy in scalars:
        copy.wait()
    lax.fori_loop(0, cycles * tiles, weigh, 0)

    brims[:, cycles * MARGIN :, :] = jnp.zeros((lanes, TILE - cycles * MARGIN, TILE), F32)
    upper = lax.broadcasted_iota(jnp.int32, (MARGIN, TILE), 0) >= MARGIN // 2

    def edge_cols(k):
        return (
            (has_left, has_right, remote(
                tall.at[k, :, pl.ds(EDGE, MARGIN)], tall.at[k, :, pl.ds(EDGE + cols, MARGIN)],
                c_send.at[k, 0], c_recv.at[k, 0], left)),
            (has_right, has_left, remote(
                tall.at[k, :, pl.ds(cols + MARGIN, MARGIN)], tall.at[k, :, pl.ds(MARGIN, MARGIN)],
                c_send.at[k, 1], c_recv.at[k, 1], right)),
        )

    def erode(k):
        def one_cycle(c, carry):
            i = c * channels + k
            received(edge_rows(i))
            for t in range(lanes):
                spread_three(corr.at[i, t], three.at[t], jnp.minimum, MARGIN, rows + 2 * MARGIN)
            for t in range(lanes):
                for b in range(halves):
                    value = spread_nine(three.at[t], jnp.minimum, EDGE + b * TILE, TILE)
                    tall[k, halves * c + b, EDGE + t * TILE : EDGE + (t + 1) * TILE, :] = value.T
                above = spread_nine(three.at[t], jnp.minimum, MARGIN, MARGIN)
                below = spread_nine(three.at[t], jnp.minimum, EDGE + rows, MARGIN)
                brims[t, pl.ds(pl.multiple_of(MARGIN * c, MARGIN), MARGIN), :] = jnp.where(upper, above, below)
            return carry

        lax.fori_loop(0, cycles, one_cycle, 0)
        for t in range(lanes):
            tall[k, halves * cycles, EDGE + t * TILE : EDGE + (t + 1) * TILE, :] = brims[t].T
        start(edge_cols(k))

    def across(k, n, place):
        spread_three(tall.at[k, n], wide1, jnp.minimum, MARGIN, cols + 2 * MARGIN)
        for at in range(MARGIN, cols + EDGE + MARGIN, CHUNK):
            size = min(CHUNK, cols + EDGE + MARGIN - at)
            wide2[at : at + size, :] = spread_nine(wide1, jnp.minimum, at, size)
        spread_three(wide2, wide1, jnp.maximum, MARGIN, cols + 2 * MARGIN)
        for t in range(lanes):
            place(t, spread_nine(wide1, jnp.maximum, EDGE + t * TILE, TILE).T)

    def keep_brims(t, value):
        brims_back[t] = value

    def hat_rows(i):
        blocks = pl.ds(1, lanes)
        return (
            (has_down, has_up, remote(
                hat.at[i, blocks, pl.ds(rows, ABOVE)], hat.at[i, blocks, pl.ds(0, ABOVE)],
                r_send.at[i, 0], r_recv.at[i, 0], down)),
            (has_up, has_down, remote(
                hat.at[i, blocks, pl.ds(ABOVE, ABOVE)], hat.at[i, blocks, pl.ds(ABOVE + rows, ABOVE)],
                r_send.at[i, 1], r_recv.at[i, 1], up)),
            (has_up, has_down, remote(next_s.at[i], next_r.at[i], n_send.at[i], n_recv.at[i], up)),
        )

    def hat_cols(i, part):
        ours, theirs = ((side_s, side_r), (corner_s, corner_r))[part]
        return (
            (has_left, has_right, remote(
                ours.at[i, 0], theirs.at[i, 0], h_send.at[i, part, 0], h_recv.at[i, part, 0], left)),
            (has_right, has_left, remote(
                ours.at[i, 1], theirs.at[i, 1], h_send.at[i, part, 1], h_recv.at[i, part, 1], right)),
        )

    def packed(first, second, side):
        early = lax.broadcasted_iota(jnp.int32, first.shape, 1) < TILE // 2
        other = pltpu.roll(second, TILE // 2, 1)
        return (jnp.where(early, first, other) if side == 0 else jnp.where(early, other, first)).astype(BF16)

    def tophat(k, c):
        i = c * channels + k
        for b in range(halves):
            def keep(t, value, b=b):
                back[t, EDGE + b * TILE : EDGE + (b + 1) * TILE, :] = value

            across(k, halves * c + b, keep)
        for t in range(lanes):
            ends = brims_back[t, pl.ds(pl.multiple_of(MARGIN * c, MARGIN), MARGIN), :]
            back[t, MARGIN:EDGE, :] = ends
            back[t, EDGE + rows : EDGE + rows + MARGIN, :] = ends
        for t in range(lanes):
            spread_three(back.at[t], three.at[t], jnp.maximum, MARGIN, rows + 2 * MARGIN)
        for t in range(lanes):
            values = []
            for b in range(halves):
                opened = spread_nine(three.at[t], jnp.maximum, EDGE + b * TILE, TILE)
                values.append(corr[i, t, EDGE + b * TILE : EDGE + (b + 1) * TILE, :] - opened)
                hat[i, t + 1, ABOVE + b * TILE : ABOVE + (b + 1) * TILE, :] = values[b].astype(BF16)
            next_s[i, t : t + 1, :] = values[0][ABOVE : ABOVE + 1].astype(BF16).astype(F32)
            if t == 0:
                side_s[i, 0] = packed(values[0], values[1], 0)
            if t == lanes - 1:
                side_s[i, 1] = packed(values[0], values[1], 1)
        start(hat_rows(i))
        start(hat_cols(i, 0))

    def corners(i):
        received(hat_rows(i))

        @pl.when(has_down)
        def _():
            first = lax.broadcasted_iota(jnp.int32, (16, TILE), 0) == 0
            for t in range(lanes):
                value = jnp.where(first, next_r[i, t : t + 1, :], 0.0)
                hat[i, t + 1, ABOVE + rows + ABOVE :, :] = value.astype(BF16)

        for side, t in ((0, 1), (1, lanes)):
            above = hat[i, t, 0:BELOW, :].astype(F32)
            below = hat[i, t, ABOVE + rows :, :].astype(F32)
            corner_s[i, side] = packed(above, below, side)
        start(hat_cols(i, 1))

    def out_copy(i):
        return pltpu.make_async_copy(reg.at[i], out.at[i // channels, i % channels], out_sem.at[i])

    def resample(i):
        for part in range(2):
            received(hat_cols(i, part))
        for side, t in ((0, lanes + 1), (1, 0)):
            middle, ends = side_r[i, side], corner_r[i, side]
            hat[i, t, ABOVE : ABOVE + TILE, :] = middle
            hat[i, t, ABOVE + TILE : ABOVE + rows, :] = pltpu.roll(middle.astype(F32), TILE // 2, 1).astype(BF16)
            hat[i, t, 0:ABOVE, :] = ends[0:ABOVE]
            hat[i, t, ABOVE + rows :, :] = pltpu.roll(ends.astype(F32), TILE // 2, 1).astype(BF16)
        c = i // channels
        span = TILE + ABOVE + BELOW
        for n in range(tiles):
            ti, tj = n // tile_cols, n % tile_cols
            window = pl.ds(ti * TILE, span)
            near = jnp.concatenate([hat[i, tj + t, window, :] for t in range(3)], axis=1)
            moved = jnp.dot(near, weights[c * tiles + n], preferred_element_type=F32)
            mixed[n] = pltpu.roll(moved, (span - ABOVE) - shifts[c, ti, 0, tj], 0)
            lower = fractions[c, ti, 0, tj].astype(F32) / 8.0
            value = mixed[n, 0:TILE, :] * (1.0 - lower) + mixed[n, 1 : TILE + 1, :] * lower
            reg[i, ti * TILE : (ti + 1) * TILE, tj * TILE : (tj + 1) * TILE] = value.astype(BF16)
        out_copy(i).start()

    part = rows // nx

    def quarter(n):
        return pl.ds(pl.multiple_of(n * part, part), part)

    def panel_copy(n, device, slot, lands):
        at = panel.at[quarter(n)]
        return remote(at, at, b_send.at[slot], b_recv.at[lands], {"cyc": device})

    def first_sends(act):
        for k in range(1, nx):
            act(panel_copy(k, k, k, 0))

    def column_sends(act):
        for k in range(1, ny):
            act(panel_copy(xx, k * nx + xx, nx + k, 0))

    def row_sends(act):
        for k in range(1, nx):
            to = lax.rem(xx + k, nx)

            def send(k=k, to=to):
                act(panel_copy(xx, yy * nx + to, nx + ny + k, k))

            pl.when(yy * nx + to > 0)(send)

    def begin(copy):
        copy.start()

    def end(copy):
        copy.wait_send()

    def own_quarter_arrives():
        panel_copy(xx, 0, 0, 0).wait_recv()

    def both(act):
        def run(c, carry):
            act(c)
            return carry

        lax.fori_loop(0, cycles, run, 0)

    def step(s, carry):
        @pl.when(s < channels)
        def _():
            erode(s)

        @pl.when((s >= 1) & (s < 1 + channels))
        def _():
            received(edge_cols(s - 1))
            across(s - 1, halves * cycles, keep_brims)
            both(lambda c: tophat(s - 1, c))

        @pl.when(s >= LAG + 1)
        def _():
            both(lambda c: resample(c * channels + s - LAG - 1))

        @pl.when((s == LAG + 1) & (cyc == 0))
        def _():
            panel[...] = reg[0]
            first_sends(begin)
            column_sends(begin)
            row_sends(begin)

        @pl.when((s == LAG + 2) & (yy == 0) & (xx > 0))
        def _():
            own_quarter_arrives()
            column_sends(begin)
            row_sends(begin)

        @pl.when((s == LAG + 3) & (yy > 0))
        def _():
            own_quarter_arrives()
            row_sends(begin)

        @pl.when((s >= LAG) & (s < LAG + channels))
        def _():
            both(lambda c: corners(c * channels + s - LAG))

        return carry

    lax.fori_loop(0, channels + LAG + 1, step, 0)

    @pl.when(cyc > 0)
    def _():
        for k in range(1, nx):
            panel_copy(lax.rem(xx + nx - k, nx), 0, 0, k).wait_recv()

    box_rows, box_cols = rows // BOX, cols // BOX
    gather = (lax.broadcasted_iota(jnp.int32, (cols, box_cols), 0) // BOX
              == lax.broadcasted_iota(jnp.int32, (cols, box_cols), 1)).astype(F32)
    spread = (lax.broadcasted_iota(jnp.int32, (box_cols, cols), 1) // BOX
              == lax.broadcasted_iota(jnp.int32, (box_cols, cols), 0)).astype(F32)
    exact = functools.partial(jnp.dot, precision=lax.Precision.HIGHEST, preferred_element_type=F32)
    area = 1.0 / (BOX * BOX)

    def stains(b):
        at = pl.ds(b * BOX, BOX)
        return [reg[c * channels, at, :].astype(F32) for c in range(cycles)] + [panel[at, :].astype(F32)]

    for b in range(box_rows):
        for n, value in enumerate(stains(b)):
            sums[n, pl.ds(b, 1), :] = jnp.sum(value, axis=0, keepdims=True)
    for n in range(cycles + 1):
        means[n] = exact(exact(sums[n], gather) * area, spread)
    for b in range(box_rows):
        centred = [value - means[n, pl.ds(b, 1), :] for n, value in enumerate(stains(b))]
        fixed = centred[cycles]
        terms = [value * fixed for value in centred] + [value * value for value in centred[:cycles]]
        for n, value in enumerate(terms):
            sums[n, pl.ds(b, 1), :] = jnp.sum(value, axis=0, keepdims=True)
    fixed_var = exact(sums[cycles], gather) * area
    for c in range(cycles):
        covar = exact(sums[c], gather) * area
        var = exact(sums[cycles + 1 + c], gather) * area
        scores[c] = covar / jnp.sqrt(var * fixed_var + 1e-06)

    def finish(i, carry):
        sent(edge_rows(i))
        sent(hat_rows(i))
        for part in range(2):
            sent(hat_cols(i, part))
        out_copy(i).wait()
        return carry

    lax.fori_loop(0, images, finish, 0)
    for k in range(channels):
        sent(edge_cols(k))
    pl.when(cyc == 0)(functools.partial(first_sends, end))
    pl.when(yy == 0)(functools.partial(column_sends, end))
    row_sends(end)


def body(sizes, raw, flat, dark, shifts, fractions):
    shifts, fractions = jnp.swapaxes(shifts, 2, 3), jnp.swapaxes(fractions, 2, 3)
    cycles, channels, rows, cols = raw.shape
    images, lanes = cycles * channels, cols // TILE
    tiles = (rows // TILE) * lanes
    dma = pltpu.SemaphoreType.DMA
    anywhere = pl.BlockSpec(memory_space=pl.ANY)
    vmem = pl.BlockSpec(memory_space=pltpu.VMEM)
    nx = math.isqrt(sizes[0])
    registered, scores = pl.pallas_call(
        functools.partial(kernel, sizes + (nx,)),
        out_shape=(
            jax.ShapeDtypeStruct(raw.shape, BF16),
            jax.ShapeDtypeStruct((cycles, rows // BOX, cols // BOX), F32),
        ),
        in_specs=[anywhere] * 5,
        out_specs=(anywhere, vmem),
        scratch_shapes=[
            pltpu.SMEM(shifts.shape, jnp.int32),
            pltpu.SMEM(fractions.shape, jnp.int32),
            pltpu.VMEM(raw.shape, BF16),
            pltpu.VMEM(flat.shape, F32),
            pltpu.VMEM(dark.shape, F32),
            pltpu.VMEM((images, lanes, rows + 2 * EDGE, TILE), F32),
            pltpu.VMEM((channels, cycles * (rows // TILE) + 1, cols + 2 * EDGE, TILE), F32),
            pltpu.VMEM((lanes, TILE, TILE), F32),
            pltpu.VMEM((lanes, TILE, TILE), F32),
            pltpu.VMEM((cols + 2 * EDGE, TILE), F32),
            pltpu.VMEM((cols + 2 * EDGE, TILE), F32),
            pltpu.VMEM((lanes, rows + 2 * EDGE, TILE), F32),
            pltpu.VMEM((lanes, rows + 2 * EDGE, TILE), F32),
            pltpu.VMEM((images, lanes + 2, ABOVE + rows + BELOW, TILE), BF16),
            pltpu.VMEM((images, 8, TILE), F32),
            pltpu.VMEM((images, 8, TILE), F32),
            pltpu.VMEM((images, 2, TILE, TILE), BF16),
            pltpu.VMEM((images, 2, TILE, TILE), BF16),
            pltpu.VMEM((images, 2, BELOW, TILE), BF16),
            pltpu.VMEM((images, 2, BELOW, TILE), BF16),
            pltpu.VMEM((tiles, TILE + ABOVE + BELOW, TILE), F32),
            pltpu.VMEM((cycles * tiles, 3 * TILE, TILE), BF16),
            pltpu.VMEM((images, rows, cols), BF16),
            pltpu.VMEM((rows, cols), BF16),
            pltpu.VMEM((2 * cycles + 1, rows // BOX, cols), F32),
            pltpu.VMEM((cycles + 1, rows // BOX, cols), F32),
            dma((channels, 3)),
            dma((2,)),
            dma((images,)),
            dma((images, 2)),
            dma((images, 2)),
            dma((channels, 2)),
            dma((channels, 2)),
            dma((images, 2)),
            dma((images, 2)),
            dma((images,)),
            dma((images,)),
            dma((images, 2, 2)),
            dma((images, 2, 2)),
            dma((2 * nx + sizes[0] // nx,)),
            dma((nx,)),
        ],
        compiler_params=pltpu.CompilerParams(
            collective_id=0, has_side_effects=True, vmem_limit_bytes=56 * 1024 * 1024
        ),
    )(raw, flat, dark, shifts, fractions)
    return registered, scores


def solution(mesh):
    sizes = (mesh.shape["cyc"], mesh.shape["row"], mesh.shape["col"])
    return jax.shard_map(
        functools.partial(body, sizes),
        mesh=mesh,
        in_specs=(
            P("cyc", None, "row", "col"),
            P(None, "row", "col"),
            P(None, "row", "col"),
            P("cyc", "row", "col", None),
            P("cyc", "row", "col", None),
        ),
        out_specs=(P("cyc", None, "row", "col"), P("cyc", "row", "col")),
        check_vma=False,
    )
```

time: 66.8 us -> 52.6 us (0.79)
  the two profiles are of different devices: /device:TPU:114 before, /device:TPU:1 now
where the time goes in v3:
time: 52.6 us; the launch traced here: 52.5 us
  Pallas kernels  48.2 us (92%)
  local copies, waits for them, and re-layouts  3.65 us (7%)
  between operations  0.65 us (1%)
    pallas_call x1, Pallas kernels, body(): pl.pallas_call(functools.partial(kernel, sizes + (nx,)), out_shape=(jax.S...  48.2 us
    unnamed x4, local copies, waits for them, and re-layouts  3.65 us

profile of v3, /device:TPU:1, one launch (start us, length us, event | category | flops | bytes accessed | tf_op | source)
XLA Modules:
  0.0 52.5 jit_solution(12435581447022502374)
XLA Ops:
  0.6 48.2 %shard_map.68 = (bf16[2,4,256,512]{3,2,1,0:T(8,128)(2,1)}, f32[2,8,16]{2,1,0:T(8,128)}) custom-call(bf16[2,4,256,512]{3,2,1,0:T(8,128)(2,1)} %raw.1, f32[4,256,512]{2,1,0:T(8,128)} %flat.1, f32[4,256,512]{2,1,0:T(8,128)} %dark.1, s32[2,2,2,4]{3,2,1,0:T(2,128)} %bitcast.2, s32[2,2,2,4]{3,2,1,0:T(2,128)} %bitcast.3), custom_call_target="tpu_custom_call" | custom-call | tf_op jit(solution)/shard_map/pallas_call | solution.py:465
  48.8 0.0 copy-start
  48.9 3.0 %copy.9 = bf16[2,4,256,512]{3,2,1,0:T(8,128)(2,1)} copy(bf16[2,4,256,512]{3,2,1,0:T(8,128)(2,1)} %get-tuple-element.4) | data formatting | bytes 4194304
  51.9 0.0 copy-done
  51.9 0.6 %copy.10 = f32[2,8,16]{2,1,0:T(8,128)} copy(f32[2,8,16]{2,1,0:T(8,128)S(1)} %copy-done) | data formatting | bytes 2048
Async XLA Ops:
  48.8 3.1 %copy-start = (f32[2,8,16]{2,1,0:T(8,128)S(1)}, f32[2,8,16]{2,1,0:T(8,128)}, u32[]{:S(2)}) copy-start(f32[2,8,16]{2,1,0:T(8,128)} %get-tuple-element.5) | copy-start | bytes 3076

commit v4 on v3

--- a/solution.py
+++ b/solution.py
@@ -53,13 +53,26 @@
     up, down = {"row": row - 1}, {"row": row + 1}
     left, right = {"col": col - 1}, {"col": col + 1}
 
+    inner = pl.ds(16, rows - 32)
+
     def in_copies(k):
         return (
-            pltpu.make_async_copy(raw.at[:, k], rawv.at[:, k], in_sem.at[k, 0]),
-            pltpu.make_async_copy(flat.at[k], flatv.at[k], in_sem.at[k, 1]),
-            pltpu.make_async_copy(dark.at[k], darkv.at[k], in_sem.at[k, 2]),
-        )
-
+            pltpu.make_async_copy(raw.at[:, k, inner], rawv.at[:, k, inner], in_sem.at[k, 0]),
+            pltpu.make_async_copy(flat.at[k, inner], flatv.at[k, inner], in_sem.at[k, 1]),
+            pltpu.make_async_copy(dark.at[k, inner], darkv.at[k, inner], in_sem.at[k, 2]),
+        )
+
+    def edge_copies(n):
+        at = pl.ds((0, rows - 16)[n], 16)
+        return (
+            pltpu.make_async_copy(raw.at[:, :, at], rawv.at[:, :, at], in_sem.at[channels + n, 0]),
+            pltpu.make_async_copy(flat.at[:, at], flatv.at[:, at], in_sem.at[channels + n, 1]),
+            pltpu.make_async_copy(dark.at[:, at], darkv.at[:, at], in_sem.at[channels + n, 2]),
+        )
+
+    for n in range(2):
+        for copy in edge_copies(n):
+            copy.start()
     for k in range(channels):
         for copy in in_copies(k):
             copy.start()
@@ -113,8 +126,6 @@
 
     expected = one(has_up) + one(has_down) + one(has_left) + one(has_right)
     expected += nx - 1 + jnp.where(yy == 0, ny - 1, 1)
-    pl.semaphore_wait(barrier, expected)
-
     def remote(source, target, send, recv, device):
         return pltpu.make_async_remote_copy(
             src_ref=source, dst_ref=target, send_sem=send, recv_sem=recv, device_id=device, device_id_type=MESH
@@ -142,27 +153,44 @@
         for sends, _, copy in moves:
             pl.when(sends)(copy.wait_send)
 
-    def correct(k, carry):
-        for copy in in_copies(k):
-            copy.wait()
-
-        def block(b, carry):
-            at = pl.ds(pl.multiple_of(b * 16, 16), 16)
-            to = pl.ds(pl.multiple_of(b * 16 + EDGE, 16), 16)
-            gain = 1.0 / flatv[k, at, :]
-            offset = darkv[k, at, :]
-            for c in range(cycles):
-                value = (rawv[c, k, at, :].astype(F32) - offset) * gain
-                for t in range(lanes):
-                    corr[c * channels + k, t, to, :] = value[:, t * TILE : (t + 1) * TILE]
-            return carry
-
-        lax.fori_loop(0, rows // 16, block, 0)
+    def correct(k, b):
+        at = pl.ds(pl.multiple_of(b * 16, 16), 16)
+        to = pl.ds(pl.multiple_of(b * 16 + EDGE, 16), 16)
+        gain = 1.0 / flatv[k, at, :]
+        offset = darkv[k, at, :]
+        for c in range(cycles):
+            value = (rawv[c, k, at, :].astype(F32) - offset) * gain
+            for t in range(lanes):
+                corr[c * channels + k, t, to, :] = value[:, t * TILE : (t + 1) * TILE]
+
+    def correct_edges(k, carry):
+        correct(k, 0)
+        correct(k, rows // 16 - 1)
+        return carry
+
+    def send_edges(k, carry):
         for c in range(cycles):
             start(edge_rows(c * channels + k))
         return carry
 
-    lax.fori_loop(0, channels, correct, 0)
+    def correct_inner(k, carry):
+        for copy in in_copies(k):
+            copy.wait()
+
+        def block(b, carry):
+            correct(k, b)
+            return carry
+
+        lax.fori_loop(1, rows // 16 - 1, block, 0)
+        return carry
+
+    for n in range(2):
+        for copy in edge_copies(n):
+            copy.wait()
+    lax.fori_loop(0, channels, correct_edges, 0)
+    pl.semaphore_wait(barrier, expected)
+    lax.fori_loop(0, channels, send_edges, 0)
+    lax.fori_loop(0, channels, correct_inner, 0)
 
     tile_rows, tile_cols = rows // TILE, cols // TILE
     tiles = tile_rows * tile_cols
@@ -298,6 +326,21 @@
     def out_copy(i):
         return pltpu.make_async_copy(reg.at[i], out.at[i // channels, i % channels], out_sem.at[i])
 
+    def blend(i, columns):
+        c = i // channels
+        span = TILE + ABOVE + BELOW
+        for n in range(tiles):
+            ti, tj = n // tile_cols, n % tile_cols
+            if tj not in columns:
+                continue
+            window = pl.ds(ti * TILE, span)
+            near = jnp.concatenate([hat[i, tj + t, window, :] for t in range(3)], axis=1)
+            moved = jnp.dot(near, weights[c * tiles + n], preferred_element_type=F32)
+            mixed[n] = pltpu.roll(moved, (span - ABOVE) - shifts[c, ti, 0, tj], 0)
+            lower = fractions[c, ti, 0, tj].astype(F32) / 8.0
+            value = mixed[n, 0:TILE, :] * (1.0 - lower) + mixed[n, 1 : TILE + 1, :] * lower
+            reg[i, ti * TILE : (ti + 1) * TILE, tj * TILE : (tj + 1) * TILE] = value.astype(BF16)
+
     def resample(i):
         for part in range(2):
             received(hat_cols(i, part))
@@ -307,17 +350,7 @@
             hat[i, t, ABOVE + TILE : ABOVE + rows, :] = pltpu.roll(middle.astype(F32), TILE // 2, 1).astype(BF16)
             hat[i, t, 0:ABOVE, :] = ends[0:ABOVE]
             hat[i, t, ABOVE + rows :, :] = pltpu.roll(ends.astype(F32), TILE // 2, 1).astype(BF16)
-        c = i // channels
-        span = TILE + ABOVE + BELOW
-        for n in range(tiles):
-            ti, tj = n // tile_cols, n % tile_cols
-            window = pl.ds(ti * TILE, span)
-            near = jnp.concatenate([hat[i, tj + t, window, :] for t in range(3)], axis=1)
-            moved = jnp.dot(near, weights[c * tiles + n], preferred_element_type=F32)
-            mixed[n] = pltpu.roll(moved, (span - ABOVE) - shifts[c, ti, 0, tj], 0)
-            lower = fractions[c, ti, 0, tj].astype(F32) / 8.0
-            value = mixed[n, 0:TILE, :] * (1.0 - lower) + mixed[n, 1 : TILE + 1, :] * lower
-            reg[i, ti * TILE : (ti + 1) * TILE, tj * TILE : (tj + 1) * TILE] = value.astype(BF16)
+        blend(i, (0, tile_cols - 1))
         out_copy(i).start()
 
     part = rows // nx
@@ -362,6 +395,41 @@
 
         lax.fori_loop(0, cycles, run, 0)
 
+    def correlate():
+        @pl.when(cyc > 0)
+        def _():
+            for k in range(1, nx):
+                panel_copy(lax.rem(xx + nx - k, nx), 0, 0, k).wait_recv()
+
+        box_rows, box_cols = rows // BOX, cols // BOX
+        gather = (lax.broadcasted_iota(jnp.int32, (cols, box_cols), 0) // BOX
+                  == lax.broadcasted_iota(jnp.int32, (cols, box_cols), 1)).astype(F32)
+        spread = (lax.broadcasted_iota(jnp.int32, (box_cols, cols), 1) // BOX
+                  == lax.broadcasted_iota(jnp.int32, (box_cols, cols), 0)).astype(F32)
+        exact = functools.partial(jnp.dot, precision=lax.Precision.HIGHEST, preferred_element_type=F32)
+        area = 1.0 / (BOX * BOX)
+
+        def stains(b):
+            at = pl.ds(b * BOX, BOX)
+            return [reg[c * channels, at, :].astype(F32) for c in range(cycles)] + [panel[at, :].astype(F32)]
+
+        for b in range(box_rows):
+            for n, value in enumerate(stains(b)):
+                sums[n, pl.ds(b, 1), :] = jnp.sum(value, axis=0, keepdims=True)
+        for n in range(cycles + 1):
+            means[n] = exact(exact(sums[n], gather) * area, spread)
+        for b in range(box_rows):
+            centred = [value - means[n, pl.ds(b, 1), :] for n, value in enumerate(stains(b))]
+            fixed = centred[cycles]
+            terms = [value * fixed for value in centred] + [value * value for value in centred[:cycles]]
+            for n, value in enumerate(terms):
+                sums[n, pl.ds(b, 1), :] = jnp.sum(value, axis=0, keepdims=True)
+        fixed_var = exact(sums[cycles], gather) * area
+        for c in range(cycles):
+            covar = exact(sums[c], gather) * area
+            var = exact(sums[cycles + 1 + c], gather) * area
+            scores[c] = covar / jnp.sqrt(var * fixed_var + 1e-06)
+
     def step(s, carry):
         @pl.when(s < channels)
         def _():
@@ -373,9 +441,20 @@
             across(s - 1, halves * cycles, keep_brims)
             both(lambda c: tophat(s - 1, c))
 
+        @pl.when((s == LAG + 2) & (yy == 0) & (xx > 0))
+        def _():
+            own_quarter_arrives()
+            column_sends(begin)
+            row_sends(begin)
+
+        @pl.when((s == LAG + 3) & (yy > 0))
+        def _():
+            own_quarter_arrives()
+            row_sends(begin)
+
         @pl.when(s >= LAG + 1)
         def _():
-            both(lambda c: resample(c * channels + s - LAG - 1))
+            resample(s - LAG - 1)
 
         @pl.when((s == LAG + 1) & (cyc == 0))
         def _():
@@ -384,58 +463,24 @@
             column_sends(begin)
             row_sends(begin)
 
-        @pl.when((s == LAG + 2) & (yy == 0) & (xx > 0))
-        def _():
-            own_quarter_arrives()
-            column_sends(begin)
-            row_sends(begin)
-
-        @pl.when((s == LAG + 3) & (yy > 0))
-        def _():
-            own_quarter_arrives()
-            row_sends(begin)
+        @pl.when(s >= LAG + 1)
+        def _():
+            def run(c, carry):
+                resample(c * channels + s - LAG - 1)
+                return carry
+
+            lax.fori_loop(1, cycles, run, 0)
+
+        pl.when(s == LAG + channels)(correlate)
 
         @pl.when((s >= LAG) & (s < LAG + channels))
         def _():
             both(lambda c: corners(c * channels + s - LAG))
+            both(lambda c: blend(c * channels + s - LAG, range(1, tile_cols - 1)))
 
         return carry
 
     lax.fori_loop(0, channels + LAG + 1, step, 0)
-
-    @pl.when(cyc > 0)
-    def _():
-        for k in range(1, nx):
-            panel_copy(lax.rem(xx + nx - k, nx), 0, 0, k).wait_recv()
-
-    box_rows, box_cols = rows // BOX, cols // BOX
-    gather = (lax.broadcasted_iota(jnp.int32, (cols, box_cols), 0) // BOX
-              == lax.broadcasted_iota(jnp.int32, (cols, box_cols), 1)).astype(F32)
-    spread = (lax.broadcasted_iota(jnp.int32, (box_cols, cols), 1) // BOX
-              == lax.broadcasted_iota(jnp.int32, (box_cols, cols), 0)).astype(F32)
-    exact = functools.partial(jnp.dot, precision=lax.Precision.HIGHEST, preferred_element_type=F32)
-    area = 1.0 / (BOX * BOX)
-
-    def stains(b):
-        at = pl.ds(b * BOX, BOX)
-        return [reg[c * channels, at, :].astype(F32) for c in range(cycles)] + [panel[at, :].astype(F32)]
-
-    for b in range(box_rows):
-        for n, value in enumerate(stains(b)):
-            sums[n, pl.ds(b, 1), :] = jnp.sum(value, axis=0, keepdims=True)
-    for n in range(cycles + 1):
-        means[n] = exact(exact(sums[n], gather) * area, spread)
-    for b in range(box_rows):
-        centred = [value - means[n, pl.ds(b, 1), :] for n, value in enumerate(stains(b))]
-        fixed = centred[cycles]
-        terms = [value * fixed for value in centred] + [value * value for value in centred[:cycles]]
-        for n, value in enumerate(terms):
-            sums[n, pl.ds(b, 1), :] = jnp.sum(value, axis=0, keepdims=True)
-    fixed_var = exact(sums[cycles], gather) * area
-    for c in range(cycles):
-        covar = exact(sums[c], gather) * area
-        var = exact(sums[cycles + 1 + c], gather) * area
-        scores[c] = covar / jnp.sqrt(var * fixed_var + 1e-06)
 
     def finish(i, carry):
         sent(edge_rows(i))
@@ -497,7 +542,7 @@
             pltpu.VMEM((rows, cols), BF16),
             pltpu.VMEM((2 * cycles + 1, rows // BOX, cols), F32),
             pltpu.VMEM((cycles + 1, rows // BOX, cols), F32),
-            dma((channels, 3)),
+            dma((channels + 2, 3)),
             dma((2,)),
             dma((images,)),
             dma((images, 2)),

time: 52.6 us -> 52 us (0.989)
  Pallas kernels: 48.2 us -> 47.6 us
    pallas_call x1, Pallas kernels: 48.2 us -> 47.6 us  [body(): pl.pallas_call(functools.partial(kernel, sizes + (nx,)), out_shape=(jax.S...]
where the time goes in v4:
time: 52 us; the launch traced here: 51.9 us
  Pallas kernels  47.6 us (92%)
  local copies, waits for them, and re-layouts  3.65 us (7%)
  between operations  0.65 us (1%)
    pallas_call x1, Pallas kernels, body(): pl.pallas_call(functools.partial(kernel, sizes + (nx,)), out_shape=(jax.S...  47.6 us
    unnamed x4, local copies, waits for them, and re-layouts  3.65 us

profile of v4, /device:TPU:1, one launch (start us, length us, event | category | flops | bytes accessed | tf_op | source)
XLA Modules:
  0.0 51.9 jit_solution(5383485282976995746)
XLA Ops:
  0.6 47.6 %shard_map.68 = (bf16[2,4,256,512]{3,2,1,0:T(8,128)(2,1)}, f32[2,8,16]{2,1,0:T(8,128)}) custom-call(bf16[2,4,256,512]{3,2,1,0:T(8,128)(2,1)} %raw.1, f32[4,256,512]{2,1,0:T(8,128)} %flat.1, f32[4,256,512]{2,1,0:T(8,128)} %dark.1, s32[2,2,2,4]{3,2,1,0:T(2,128)} %bitcast.2, s32[2,2,2,4]{3,2,1,0:T(2,128)} %bitcast.3), custom_call_target="tpu_custom_call" | custom-call | tf_op jit(solution)/shard_map/pallas_call | solution.py:510
  48.2 0.0 copy-start
  48.3 3.0 %copy.9 = bf16[2,4,256,512]{3,2,1,0:T(8,128)(2,1)} copy(bf16[2,4,256,512]{3,2,1,0:T(8,128)(2,1)} %get-tuple-element.4) | data formatting | bytes 4194304
  51.3 0.0 copy-done
  51.3 0.6 %copy.10 = f32[2,8,16]{2,1,0:T(8,128)} copy(f32[2,8,16]{2,1,0:T(8,128)S(1)} %copy-done) | data formatting | bytes 2048
Async XLA Ops:
  48.2 3.1 %copy-start = (f32[2,8,16]{2,1,0:T(8,128)S(1)}, f32[2,8,16]{2,1,0:T(8,128)}, u32[]{:S(2)}) copy-start(f32[2,8,16]{2,1,0:T(8,128)} %get-tuple-element.5) | copy-start | bytes 3076
